TPU v7x, 512 devices: a whole 4x4x16 slice. The times are simulated.
512 devices in a mesh: seq: 32 (over y, x, core), head: 16 (over z).
Axes of the slice: x: 4, y: 4, z: 16, core: 2. Of those that a mesh axis runs over, the one named last changes fastest.
Arguments:
- shared_qk: bfloat16 [65536, 2048], P('seq', 'head'), may hold values from -6 to 6
- values: bfloat16 [65536, 2048], P('seq', 'head'), may hold values from -6 to 6
- cotangent: bfloat16 [65536, 2048], P('seq', 'head'), may hold values from -6 to 6
- cluster_ids: int32 [512], replicated, may hold values from 0 to 511, as said below
- neighbour: int32 [512], replicated, may hold values from -1 to 511, as said below
Outputs:
- grad_qk: bfloat16 [65536, 2048], P('seq', 'head')
- grad_values: bfloat16 [65536, 2048], P('seq', 'head')
Inputs may be any that keep to these rules, and one draw needn't show every extreme that they name: `cluster_ids`: clusters g * 16 to (g + 1) * 16 - 1 form group g. The 16 blocks of one seq index go to 16 groups, exactly 1 to each; every group receives exactly 16 blocks. A cluster holds at most 2 blocks, and in each group as many clusters hold 2 blocks as hold none. `neighbour`: each entry is -1 or the cluster 1 ids further along in the same group, cyclically.
All inputs are finite; a program needn't handle non-finite values.
Results may differ from a plain program's by a relative error of at most 0.0094.
Values may be sent and summed in bfloat16 or wider, within the bound.
No kernel may reach another device: no remote copies, remote signals or barrier semaphores. Data moves between devices by JAX's collectives and lax.ppermute only.
A program may use at most 64 MiB of HBM per device.

v0:
```python
import math

import jax
import jax.numpy as jnp
from jax import lax
from jax.sharding import PartitionSpec as P

BLOCK = 128
DH = 128
CAPC = 2


def attend(
    query_local_rows, value_own, cotangent_local_rows, query_near, value_near, own_ok, near_ok
):
    row_count = query_local_rows.shape[1]
    score_scale_factor = 1.0 / math.sqrt(query_local_rows.shape[2])
    key_matrix_rows = jnp.concatenate([query_local_rows, query_near], axis=1)
    value_matrix_rows = jnp.concatenate([value_own, value_near], axis=1)
    logit_scores = (
        jnp.einsum(
            "ylz,yez->yle", query_local_rows, key_matrix_rows, preferred_element_type=jnp.float32
        )
        * score_scale_factor
    )
    key_ok = jnp.concatenate([own_ok, near_ok], axis=1)
    not_self = jnp.arange(2 * row_count)[None, :] != jnp.arange(row_count)[:, None]
    allowed = key_ok[:, None, :] & not_self[None, :, :]
    logit_scores = jnp.where(allowed, logit_scores, -1e30)
    row_max = jnp.max(logit_scores, axis=2, keepdims=True)
    weight = jnp.where(allowed, jnp.exp(logit_scores - row_max), 0.0)
    denominator = jnp.sum(weight, axis=2, keepdims=True) + jnp.where(own_ok, 0.0, 1.0)[:, :, None]
    probs = weight / denominator
    probabilities_reduced = probs.astype(jnp.bfloat16)
    attended_output = jnp.einsum(
        "ynp,ypm->ynm", probabilities_reduced, value_matrix_rows, preferred_element_type=jnp.float32
    )
    delta = jnp.sum(
        cotangent_local_rows.astype(jnp.float32) * attended_output, axis=2, keepdims=True
    )
    probability_gradient = jnp.einsum(
        "ylz,yez->yle", cotangent_local_rows, value_matrix_rows, preferred_element_type=jnp.float32
    )
    score_gradient = (probs * (probability_gradient - delta) * score_scale_factor).astype(
        jnp.bfloat16
    )
    query_gradient = jnp.einsum(
        "ynp,ypm->ynm", score_gradient, key_matrix_rows, preferred_element_type=jnp.float32
    )
    key_gradient = jnp.einsum(
        "eap,eas->eps", score_gradient, query_local_rows, preferred_element_type=jnp.float32
    )
    value_gradient = jnp.einsum(
        "eap,eas->eps",
        probabilities_reduced,
        cotangent_local_rows,
        preferred_element_type=jnp.float32,
    )
    own_qk = (query_gradient + key_gradient[:, :row_count]).astype(jnp.bfloat16)
    own_v = value_gradient[:, :row_count].astype(jnp.bfloat16)
    return (
        own_qk,
        own_v,
        key_gradient[:, row_count:].astype(jnp.bfloat16),
        value_gradient[:, row_count:].astype(jnp.bfloat16),
    )


def attend_items(items):
    return attend(items[0], items[1], items[2], items[3], items[4], items[5], items[6])


def locate(target, wanted, payload, missing):
    hits = target[None, :] == wanted[:, None]
    found = jnp.sum(jnp.where(hits, payload[None, :], 0), axis=1)
    return jnp.where(jnp.any(hits, axis=1), found, missing)


def block_tables(cluster_ids, per_source, group_size):
    count = cluster_ids.shape[0]
    indices = jnp.arange(count, dtype=jnp.int32)
    earlier = indices[None, :] < indices[:, None]
    source = indices // per_source
    group = cluster_ids // group_size
    same_pair = (source[:, None] == source[None, :]) & (group[:, None] == group[None, :])
    pair_slot = jnp.sum((earlier & same_pair).astype(jnp.int32), axis=1)
    same_cluster = cluster_ids[:, None] == cluster_ids[None, :]
    position = jnp.sum((earlier & same_cluster).astype(jnp.int32), axis=1)
    return (source, group, pair_slot, position)


def to_items(field):
    count, row_count, head_count, width = field.shape
    return field.transpose(0, 2, 1, 3).reshape(count * head_count, row_count, width)


def from_items(field, count, head_count):
    row_count, width = (field.shape[1], field.shape[2])
    return field.reshape(count, head_count, row_count, width).transpose(0, 2, 1, 3)


def cluster_masks(cluster_ids, neighbour, local, near, slot_rows):
    sizes_own = jnp.sum((cluster_ids[None, :] == local[:, None]).astype(jnp.int32), axis=1)
    sizes_near = jnp.sum((cluster_ids[None, :] == near[:, None]).astype(jnp.int32), axis=1)
    all_ids = jnp.arange(neighbour.shape[0], dtype=jnp.int32)
    flagged = jnp.any((all_ids[None, :] == local[:, None]) & (neighbour[None, :] >= 0), axis=1)
    slot_of_row = (jnp.arange(slot_rows) // BLOCK)[None, :]
    own_ok = slot_of_row < sizes_own[:, None]
    near_ok = (slot_of_row < sizes_near[:, None]) & flagged[:, None]
    return (own_ok, near_ok)


def run_attention(query_tiles, value_tiles, cot_tiles, query_near, value_near, own_ok, near_ok):
    count, slot_rows, head_count = (
        query_tiles.shape[0],
        query_tiles.shape[1],
        query_tiles.shape[2],
    )
    item_count = count * head_count
    per_turn = math.gcd(item_count, max(1, 1024 // slot_rows))
    turns = item_count // per_turn

    def split_turns(field):
        return field.reshape((turns, per_turn) + field.shape[1:])

    own_mask = jnp.repeat(own_ok, head_count, axis=0)
    near_mask = jnp.repeat(near_ok, head_count, axis=0)
    pieces = (
        to_items(query_tiles),
        to_items(value_tiles),
        to_items(cot_tiles),
        to_items(query_near),
        to_items(value_near),
        own_mask,
        near_mask,
    )
    results = lax.map(attend_items, tuple((split_turns(piece) for piece in pieces)))
    return tuple(
        (
            from_items(result.reshape((item_count,) + result.shape[2:]), count, head_count)
            for result in results
        )
    )


def per_device(shared_qk, values, cotangent, cluster_ids, neighbour):
    n_seq = lax.axis_size("seq")
    n_head = lax.axis_size("head")
    seq_index = lax.axis_index("seq")
    token_count, lane_count = shared_qk.shape
    per_source = token_count // BLOCK
    heads_here = lane_count // DH
    cluster_count = neighbour.shape[0]
    group_size = cluster_count // n_seq
    per_owner = group_size // n_head
    slot_count = max(1, 2 * per_source // n_seq)
    slot_rows = CAPC * BLOCK
    tile_count = group_size * CAPC
    arrive_count = n_seq * slot_count
    source, group, pair_slot, position = block_tables(cluster_ids, per_source, group_size)
    send_key = group * slot_count + pair_slot
    local_key = lax.dynamic_slice_in_dim(send_key, seq_index * per_source, per_source)
    local_ids = jnp.arange(per_source, dtype=jnp.int32)
    send_index = locate(local_key, jnp.arange(arrive_count, dtype=jnp.int32), local_ids, per_source)

    def outgoing(field):
        blocks = field.reshape(per_source, BLOCK, lane_count)
        blocks = jnp.concatenate([blocks, jnp.zeros((1, BLOCK, lane_count), field.dtype)], axis=0)
        return jnp.take(blocks, send_index, axis=0).reshape(n_seq, slot_count, BLOCK, lane_count)

    arrived = (
        lax.all_to_all(outgoing(shared_qk), "seq", split_axis=0, concat_axis=0, tiled=True),
        lax.all_to_all(outgoing(values), "seq", split_axis=0, concat_axis=0, tiled=True),
        lax.all_to_all(outgoing(cotangent), "seq", split_axis=0, concat_axis=0, tiled=True),
    )
    arrive_slot = jnp.where(group == seq_index, source * slot_count + pair_slot, arrive_count)
    tile_key = cluster_ids * CAPC + position - seq_index * tile_count
    tile_ids = jnp.arange(tile_count, dtype=jnp.int32)
    tile_index = locate(tile_key, tile_ids, arrive_slot, arrive_count)
    back_index = locate(tile_index, jnp.arange(arrive_count, dtype=jnp.int32), tile_ids, tile_count)

    def to_group_tiles(piece):
        flat = piece.reshape(arrive_count, BLOCK, lane_count)
        flat = jnp.concatenate([flat, jnp.zeros((1, BLOCK, lane_count), piece.dtype)], axis=0)
        return jnp.take(flat, tile_index, axis=0)

    qk_group = to_group_tiles(arrived[0])
    value_group = to_group_tiles(arrived[1])
    cot_group = to_group_tiles(arrived[2])
    group_base = seq_index * group_size
    local = group_base + jnp.arange(group_size, dtype=jnp.int32)
    near = group_base + (local - group_base + per_owner) % group_size
    own_ok, near_ok = cluster_masks(cluster_ids, neighbour, local, near, slot_rows)
    tile_shape = (group_size, slot_rows, heads_here, DH)
    query_tiles = qk_group.reshape(tile_shape)
    value_tiles = value_group.reshape(tile_shape)
    cot_tiles = cot_group.reshape(tile_shape)
    query_near = jnp.roll(query_tiles, -per_owner, axis=0)
    value_near = jnp.roll(value_tiles, -per_owner, axis=0)
    own_qk, own_v, part_qk, part_v = run_attention(
        query_tiles, value_tiles, cot_tiles, query_near, value_near, own_ok, near_ok
    )
    flat_shape = (tile_count, BLOCK, lane_count)
    total_qk = (
        own_qk.reshape(flat_shape).astype(jnp.float32)
        + jnp.roll(part_qk, per_owner, axis=0).reshape(flat_shape).astype(jnp.float32)
    ).astype(jnp.bfloat16)
    total_v = (
        own_v.reshape(flat_shape).astype(jnp.float32)
        + jnp.roll(part_v, per_owner, axis=0).reshape(flat_shape).astype(jnp.float32)
    ).astype(jnp.bfloat16)

    def returning(tiles):
        flat = jnp.concatenate([tiles, jnp.zeros((1, BLOCK, lane_count), tiles.dtype)], axis=0)
        return jnp.take(flat, back_index, axis=0).reshape(n_seq, slot_count, BLOCK, lane_count)

    home_qk, home_v = (
        lax.all_to_all(returning(total_qk), "seq", split_axis=0, concat_axis=0, tiled=True),
        lax.all_to_all(returning(total_v), "seq", split_axis=0, concat_axis=0, tiled=True),
    )
    grad_qk = jnp.take(home_qk.reshape(arrive_count, BLOCK, lane_count), local_key, axis=0).reshape(
        token_count, lane_count
    )
    grad_values = jnp.take(
        home_v.reshape(arrive_count, BLOCK, lane_count), local_key, axis=0
    ).reshape(token_count, lane_count)
    return (grad_qk, grad_values)


def solution(mesh):
    in_specs = (P("seq", "head"), P("seq", "head"), P("seq", "head"), P(), P())
    out_specs = (P("seq", "head"), P("seq", "head"))
    return jax.shard_map(
        per_device, mesh=mesh, in_specs=in_specs, out_specs=out_specs, check_vma=False
    )
```

profile of v0, /device:TPU:1, one launch (start us, length us, event | category | flops | bytes accessed | tf_op | source)
XLA Modules:
  0.0 186.3 jit_solution(16932387786029355266)
XLA Ops:
  0.6 1.0 convert_reduce_fusion
  1.6 0.7 add_subtract_fusion
  3.0 1.1 concatenate.47
  4.1 1.1 concatenate.52
  5.2 0.7 gather_fusion
  5.9 0.7 gather_fusion.4
  7.0 1.7 gather_fusion.2
  8.7 2.9 %select_bitcast_fusion.2 = (bf16[32,1,128,128]{3,2,1,0:T(8,128)(2,1)}, bf16[32,1,128,128]{3,2,1,0:T(8,128)(2,1)S(1)}, bf16[32,1,128,128]{3,2,1,0:T(8,128)(2,1)}) fusion(bf16[32,128,128]{2,1,0:T(8,128)(2,1)S(1)} %gather_fusion.4, pred[32]{0:T(512)(128)(4,1)S(1)} %get-tuple-element.106, bf16[32,128,128]{2,1,0:T(8,128)(2,1)} %gather_fusion.2, ...), kind=kLoop, calls=%fused_computation.70 | loop fusion | flops 1572864 | bytes 6291488 | tf_op jit(solution)/shard_map/reshape | solution.py:169
  11.7 26.9 %all_to_all.25 = bf16[32,1,128,128]{3,2,1,0:T(8,128)(2,1)S(1)} all-to-all(bf16[32,1,128,128]{3,2,1,0:T(8,128)(2,1)S(1)} %get-tuple-element.127), channel_id=1, replica_groups=mesh['seq'=32,'head'=16] {'seq'}, dimensions={0} | all-to-all | bytes 2097152 | tf_op jit(solution)/shard_map/all_to_all | solution.py:174
  38.6 4.0 %all-to-all-start = ((bf16[32,1,128,128]{3,2,1,0:T(8,128)(2,1)}), bf16[32,1,128,128]{3,2,1,0:T(8,128)(2,1)S(1)}, u32[]{:S(2)}, u32[]{:S(2)}) async-start(bf16[32,1,128,128]{3,2,1,0:T(8,128)(2,1)} %get-tuple-element.128), calls=%async_computation | async-start | bytes 2097152 | tf_op jit(solution)/shard_map/all_to_all | solution.py:172
  43.1 16.8 %all-to-all-done = bf16[32,1,128,128]{3,2,1,0:T(8,128)(2,1)S(1)} async-done(((bf16[32,1,128,128]{3,2,1,0:T(8,128)(2,1)}), bf16[32,1,128,128]{3,2,1,0:T(8,128)(2,1)S(1)}, u32[]{:S(2)}, u32[]{:S(2)}) %all-to-all-start) | async-done | bytes 1048608 | tf_op jit(solution)/shard_map/all_to_all | solution.py:172
  59.9 4.6 %all-to-all-start.2 = ((bf16[32,1,128,128]{3,2,1,0:T(8,128)(2,1)}), bf16[32,1,128,128]{3,2,1,0:T(8,128)(2,1)}, u32[]{:S(2)}, u32[]{:S(2)}) async-start(bf16[32,1,128,128]{3,2,1,0:T(8,128)(2,1)} %get-tuple-element.126), calls=%async_computation.2 | async-start | bytes 2097152 | tf_op jit(solution)/shard_map/all_to_all | solution.py:173
  65.6 0.8 gather_fusion.1
  66.4 1.7 gather_fusion.3
  68.0 13.8 %all-to-all-done.2 = bf16[32,1,128,128]{3,2,1,0:T(8,128)(2,1)} async-done(((bf16[32,1,128,128]{3,2,1,0:T(8,128)(2,1)}), bf16[32,1,128,128]{3,2,1,0:T(8,128)(2,1)}, u32[]{:S(2)}, u32[]{:S(2)}) %all-to-all-start.2) | async-done | bytes 1048608 | tf_op jit(solution)/shard_map/all_to_all | solution.py:173
  81.9 1.3 concatenate.53
  83.2 1.7 gather_fusion.5
  84.9 3.0 %broadcast_select_fusion = (bf16[32,128,128]{2,1,0:T(8,128)(2,1)S(1)}, bf16[32,128,128]{2,1,0:T(8,128)(2,1)}, bf16[32,128,128]{2,1,0:T(8,128)(2,1)S(1)}) fusion(bf16[32,128,128]{2,1,0:T(8,128)(2,1)} %gather_fusion.5, pred[32]{0:T(512)(128)(4,1)S(1)} %get-tuple-element.104, bf16[32,128,128]{2,1,0:T(8,128)(2,1)} %gather_fusion.3, ...), kind=kLoop, calls=%fused_computation.78 | loop fusion | flops 1572864 | bytes 6291488 | tf_op jit(solution)/shard_map/jit(_take)/select_n | solution.py:185
  88.1 1.1 pad_maximum_fusion.13
  89.2 1.1 pad_maximum_fusion.12
  90.3 43.9 %while.16 = (s32[]{:T(128)}, bf16[4,4,256,128]{3,2,1,0:T(8,128)(2,1)}, bf16[4,4,256,128]{3,2,1,0:T(8,128)(2,1)}, bf16[4,4,256,128]{3,2,1,0:T(8,128)(2,1)}, bf16[...) while((s32[]{:T(128)}, ...), condition=%wide.region_13.16_spmd, body=%wide.region_9.15_spmd.sunk | while | flops 818941440 | bytes 33598700 | solution.py:137
  90.4 1.0 dynamic-slice_bitcast_fusion.12
  91.4 1.0 dynamic-slice_bitcast_fusion.17
  92.3 2.4 %fusion.75 = (f32[4,256]{1,0:T(4,128)S(1)}, f32[4,256,512]{2,1,0:T(8,128)}) fusion(pred[256,512]{1,0:T(8,128)(4,1)S(1)} %iota_compare_fusion.7, pred[4,512]{1,0:T(4,128)(4,1)S(1)} %pad_add_fusion.2, bf16[4,256,128]{2,1,0:T(8,128)(2,1)S(1)} %dynamic-slice_bitcast_fusion.16, bf16[4,256,128]{2,1,0:T(8,128)(2,1)S(1)} %dynamic-slice_bitcast_fusion.17), kind=kOutput, calls=%fused_computation.139.clone.1 | convolution fusion | flops 138936832 | bytes 2758656 | tf_op jit(solution)/shard_map/while/body/eval_jaxpr/sub | solution.py:31
  94.8 2.3 %fusion.76 = f32[4,256]{1,0:T(4,128)S(1)} fusion(bf16[4,256,128]{2,1,0:T(8,128)(2,1)S(1)} %dynamic-slice_bitcast_fusion.12, bf16[4,256,128]{2,1,0:T(8,128)(2,1)S(1)} %dynamic-slice_bitcast_fusion.13, bf16[4,4,256,128]{3,2,1,0:T(8,128)(2,1)} %get-tuple-element.250, s32[]{:T(128)S(6)} %copy.36, f32[4,256,512]{2,1,0:T(8,128)} %get-tuple-element.210, ...), kind=kOutput, calls=%fused_computation.19.clone.1 | convolution fusion | flops 136707072 | bytes 2891780 | tf_op jit(solution)/shard_map/while/body/eval_jaxpr/ynp,ypm->ynm/dot_general | solution.py:35
  97.9 0.7 convolution_convert_fusion.2
  98.6 0.5 fusion.77
  99.1 1.1 fusion.78
  100.3 1.0 fusion.79
  101.3 1.0 dynamic-slice_bitcast_fusion.12
  102.3 1.0 dynamic-slice_bitcast_fusion.17
  103.3 2.4 %fusion.75 = (f32[4,256]{1,0:T(4,128)S(1)}, f32[4,256,512]{2,1,0:T(8,128)}) fusion(pred[256,512]{1,0:T(8,128)(4,1)S(1)} %iota_compare_fusion.7, pred[4,512]{1,0:T(4,128)(4,1)S(1)} %pad_add_fusion.2, bf16[4,256,128]{2,1,0:T(8,128)(2,1)S(1)} %dynamic-slice_bitcast_fusion.16, bf16[4,256,128]{2,1,0:T(8,128)(2,1)S(1)} %dynamic-slice_bitcast_fusion.17), kind=kOutput, calls=%fused_computation.139.clone.1 | convolution fusion | flops 138936832 | bytes 2758656 | tf_op jit(solution)/shard_map/while/body/eval_jaxpr/sub | solution.py:31
  105.8 2.3 %fusion.76 = f32[4,256]{1,0:T(4,128)S(1)} fusion(bf16[4,256,128]{2,1,0:T(8,128)(2,1)S(1)} %dynamic-slice_bitcast_fusion.12, bf16[4,256,128]{2,1,0:T(8,128)(2,1)S(1)} %dynamic-slice_bitcast_fusion.13, bf16[4,4,256,128]{3,2,1,0:T(8,128)(2,1)} %get-tuple-element.250, s32[]{:T(128)S(6)} %copy.36, f32[4,256,512]{2,1,0:T(8,128)} %get-tuple-element.210, ...), kind=kOutput, calls=%fused_computation.19.clone.1 | convolution fusion | flops 136707072 | bytes 2891780 | tf_op jit(solution)/shard_map/while/body/eval_jaxpr/ynp,ypm->ynm/dot_general | solution.py:35
  108.9 0.7 convolution_convert_fusion.2
  110.1 1.2 fusion.78
  111.3 0.9 fusion.79
  112.3 1.0 dynamic-slice_bitcast_fusion.12
  113.3 1.0 dynamic-slice_bitcast_fusion.17
  114.3 2.4 %fusion.75 = (f32[4,256]{1,0:T(4,128)S(1)}, f32[4,256,512]{2,1,0:T(8,128)}) fusion(pred[256,512]{1,0:T(8,128)(4,1)S(1)} %iota_compare_fusion.7, pred[4,512]{1,0:T(4,128)(4,1)S(1)} %pad_add_fusion.2, bf16[4,256,128]{2,1,0:T(8,128)(2,1)S(1)} %dynamic-slice_bitcast_fusion.16, bf16[4,256,128]{2,1,0:T(8,128)(2,1)S(1)} %dynamic-slice_bitcast_fusion.17), kind=kOutput, calls=%fused_computation.139.clone.1 | convolution fusion | flops 138936832 | bytes 2758656 | tf_op jit(solution)/shard_map/while/body/eval_jaxpr/sub | solution.py:31
  116.7 2.3 %fusion.76 = f32[4,256]{1,0:T(4,128)S(1)} fusion(bf16[4,256,128]{2,1,0:T(8,128)(2,1)S(1)} %dynamic-slice_bitcast_fusion.12, bf16[4,256,128]{2,1,0:T(8,128)(2,1)S(1)} %dynamic-slice_bitcast_fusion.13, bf16[4,4,256,128]{3,2,1,0:T(8,128)(2,1)} %get-tuple-element.250, s32[]{:T(128)S(6)} %copy.36, f32[4,256,512]{2,1,0:T(8,128)} %get-tuple-element.210, ...), kind=kOutput, calls=%fused_computation.19.clone.1 | convolution fusion | flops 136707072 | bytes 2891780 | tf_op jit(solution)/shard_map/while/body/eval_jaxpr/ynp,ypm->ynm/dot_general | solution.py:35
  119.9 0.7 convolution_convert_fusion.2
  120.6 0.5 fusion.77
  121.1 1.2 fusion.78
  122.3 0.9 fusion.79
  123.2 1.0 dynamic-slice_bitcast_fusion.12
  124.3 1.0 dynamic-slice_bitcast_fusion.17
  125.2 2.4 %fusion.75 = (f32[4,256]{1,0:T(4,128)S(1)}, f32[4,256,512]{2,1,0:T(8,128)}) fusion(pred[256,512]{1,0:T(8,128)(4,1)S(1)} %iota_compare_fusion.7, pred[4,512]{1,0:T(4,128)(4,1)S(1)} %pad_add_fusion.2, bf16[4,256,128]{2,1,0:T(8,128)(2,1)S(1)} %dynamic-slice_bitcast_fusion.16, bf16[4,256,128]{2,1,0:T(8,128)(2,1)S(1)} %dynamic-slice_bitcast_fusion.17), kind=kOutput, calls=%fused_computation.139.clone.1 | convolution fusion | flops 138936832 | bytes 2758656 | tf_op jit(solution)/shard_map/while/body/eval_jaxpr/sub | solution.py:31
  127.7 2.3 %fusion.76 = f32[4,256]{1,0:T(4,128)S(1)} fusion(bf16[4,256,128]{2,1,0:T(8,128)(2,1)S(1)} %dynamic-slice_bitcast_fusion.12, bf16[4,256,128]{2,1,0:T(8,128)(2,1)S(1)} %dynamic-slice_bitcast_fusion.13, bf16[4,4,256,128]{3,2,1,0:T(8,128)(2,1)} %get-tuple-element.250, s32[]{:T(128)S(6)} %copy.36, f32[4,256,512]{2,1,0:T(8,128)} %get-tuple-element.210, ...), kind=kOutput, calls=%fused_computation.19.clone.1 | convolution fusion | flops 136707072 | bytes 2891780 | tf_op jit(solution)/shard_map/while/body/eval_jaxpr/ynp,ypm->ynm/dot_general | solution.py:35
  130.8 0.7 convolution_convert_fusion.2
  132.0 1.2 fusion.78
  133.2 0.9 fusion.79
  134.1 0.9 slice.97
  135.1 1.3 slice.98
  136.6 1.0 copy-done.1
  138.3 1.0 copy-done.2
  139.9 0.8 gather_fusion.8
  140.6 0.7 gather_fusion.6
  141.4 1.2 select_bitcast_fusion
  142.7 20.6 %all_to_all.26 = bf16[32,1,128,128]{3,2,1,0:T(8,128)(2,1)S(1)} all-to-all(bf16[32,1,128,128]{3,2,1,0:T(8,128)(2,1)S(1)} %get-tuple-element.121), channel_id=1, replica_groups=mesh['seq'=32,'head'=16] {'seq'}, dimensions={0} | all-to-all | bytes 2097152 | tf_op jit(solution)/shard_map/all_to_all | solution.py:219
  163.3 4.0 %all-to-all-start.3 = ((bf16[32,1,128,128]{3,2,1,0:T(8,128)(2,1)}), bf16[32,1,128,128]{3,2,1,0:T(8,128)(2,1)S(1)}, u32[]{:S(2)}, u32[]{:S(2)}) async-start(bf16[32,1,128,128]{3,2,1,0:T(8,128)(2,1)} %get-tuple-element.122), calls=%async_computation.3 | async-start | bytes 2097152 | tf_op jit(solution)/shard_map/all_to_all | solution.py:218
  167.3 0.6 gather_fusion.9
  167.9 16.6 %all-to-all-done.3 = bf16[32,1,128,128]{3,2,1,0:T(8,128)(2,1)S(1)} async-done(((bf16[32,1,128,128]{3,2,1,0:T(8,128)(2,1)}), bf16[32,1,128,128]{3,2,1,0:T(8,128)(2,1)S(1)}, u32[]{:S(2)}, u32[]{:S(2)}) %all-to-all-start.3) | async-done | bytes 1048608 | tf_op jit(solution)/shard_map/all_to_all | solution.py:218
  184.5 0.6 gather_fusion.7
  185.2 1.1 broadcast_select_fusion.3
  (106 shorter events, 8.7 us)
Async XLA Ops:
  5.9 1.0 copy-start.4
  11.7 31.2 %copy-start.5 = (s32[512]{0:T(512)S(1)}, s32[512]{0:T(512)}, u32[]{:S(2)}) copy-start(s32[512]{0:T(512)} %param.16) | copy-start | bytes 6148
  11.7 31.4 %copy-start.6 = (s32[512]{0:T(512)S(1)}, s32[512]{0:T(512)}, u32[]{:S(2)}) copy-start(s32[512]{0:T(512)} %param.17) | copy-start | bytes 6148
  38.6 21.3 %all-to-all-start = ((bf16[32,1,128,128]{3,2,1,0:T(8,128)(2,1)}), bf16[32,1,128,128]{3,2,1,0:T(8,128)(2,1)S(1)}, u32[]{:S(2)}, u32[]{:S(2)}) async-start(bf16[32,1,128,128]{3,2,1,0:T(8,128)(2,1)} %get-tuple-element.128), calls=%async_computation | async-start | bytes 2097152 | tf_op jit(solution)/shard_map/all_to_all | solution.py:172
  59.9 22.0 %all-to-all-start.2 = ((bf16[32,1,128,128]{3,2,1,0:T(8,128)(2,1)}), bf16[32,1,128,128]{3,2,1,0:T(8,128)(2,1)}, u32[]{:S(2)}, u32[]{:S(2)}) async-start(bf16[32,1,128,128]{3,2,1,0:T(8,128)(2,1)} %get-tuple-element.126), calls=%async_computation.2 | async-start | bytes 2097152 | tf_op jit(solution)/shard_map/all_to_all | solution.py:173
  94.8 2.3 %copy-start = (bf16[4,4,256,128]{3,2,1,0:T(8,128)(2,1)S(1)}, bf16[4,4,256,128]{3,2,1,0:T(8,128)(2,1)}, u32[]{:S(2)}) copy-start(bf16[4,4,256,128]{3,2,1,0:T(8,128)(2,1)} %get-tuple-element.250) | copy-start | bytes 3145732 | tf_op jit(solution)/shard_map/while
  94.8 2.6 %copy-start.7 = (f32[4,256,512]{2,1,0:T(8,128)S(1)}, f32[4,256,512]{2,1,0:T(8,128)}, u32[]{:S(2)}) copy-start(f32[4,256,512]{2,1,0:T(8,128)} %get-tuple-element.210) | copy-start | bytes 6291460 | tf_op jit(solution)/shard_map/while
  105.8 2.3 %copy-start = (bf16[4,4,256,128]{3,2,1,0:T(8,128)(2,1)S(1)}, bf16[4,4,256,128]{3,2,1,0:T(8,128)(2,1)}, u32[]{:S(2)}) copy-start(bf16[4,4,256,128]{3,2,1,0:T(8,128)(2,1)} %get-tuple-element.250) | copy-start | bytes 3145732 | tf_op jit(solution)/shard_map/while
  105.8 2.6 %copy-start.7 = (f32[4,256,512]{2,1,0:T(8,128)S(1)}, f32[4,256,512]{2,1,0:T(8,128)}, u32[]{:S(2)}) copy-start(f32[4,256,512]{2,1,0:T(8,128)} %get-tuple-element.210) | copy-start | bytes 6291460 | tf_op jit(solution)/shard_map/while
  116.7 2.3 %copy-start = (bf16[4,4,256,128]{3,2,1,0:T(8,128)(2,1)S(1)}, bf16[4,4,256,128]{3,2,1,0:T(8,128)(2,1)}, u32[]{:S(2)}) copy-start(bf16[4,4,256,128]{3,2,1,0:T(8,128)(2,1)} %get-tuple-element.250) | copy-start | bytes 3145732 | tf_op jit(solution)/shard_map/while
  116.7 2.6 %copy-start.7 = (f32[4,256,512]{2,1,0:T(8,128)S(1)}, f32[4,256,512]{2,1,0:T(8,128)}, u32[]{:S(2)}) copy-start(f32[4,256,512]{2,1,0:T(8,128)} %get-tuple-element.210) | copy-start | bytes 6291460 | tf_op jit(solution)/shard_map/while
  127.7 2.3 %copy-start = (bf16[4,4,256,128]{3,2,1,0:T(8,128)(2,1)S(1)}, bf16[4,4,256,128]{3,2,1,0:T(8,128)(2,1)}, u32[]{:S(2)}) copy-start(bf16[4,4,256,128]{3,2,1,0:T(8,128)(2,1)} %get-tuple-element.250) | copy-start | bytes 3145732 | tf_op jit(solution)/shard_map/while
  127.7 2.6 %copy-start.7 = (f32[4,256,512]{2,1,0:T(8,128)S(1)}, f32[4,256,512]{2,1,0:T(8,128)}, u32[]{:S(2)}) copy-start(f32[4,256,512]{2,1,0:T(8,128)} %get-tuple-element.210) | copy-start | bytes 6291460 | tf_op jit(solution)/shard_map/while
  134.1 2.2 %copy-start.3 = (bf16[4,4,256,128]{3,2,1,0:T(8,128)(2,1)S(1)}, bf16[4,4,256,128]{3,2,1,0:T(8,128)(2,1)}, u32[]{:S(2)}) copy-start(bf16[4,4,256,128]{3,2,1,0:T(8,128)(2,1)} %get-tuple-element.71) | copy-start | bytes 3145732
  136.4 1.2 copy-start.1
  138.1 1.2 copy-start.2
  163.3 21.3 %all-to-all-start.3 = ((bf16[32,1,128,128]{3,2,1,0:T(8,128)(2,1)}), bf16[32,1,128,128]{3,2,1,0:T(8,128)(2,1)S(1)}, u32[]{:S(2)}, u32[]{:S(2)}) async-start(bf16[32,1,128,128]{3,2,1,0:T(8,128)(2,1)} %get-tuple-element.122), calls=%async_computation.3 | async-start | bytes 2097152 | tf_op jit(solution)/shard_map/all_to_all | solution.py:218
where the time goes:
time: 187 us; the launch traced here: 186 us
  blocking collectives  47.6 us (25%)
  waiting for transfers between devices  47.2 us (25%)
  local copies, waits for them, and re-layouts  32.1 us (17%)
  matrix products  30.5 us (16%)
  other arithmetic  15 us (8%)
  starting transfers between devices  12.6 us (7%)
    all_to_all x1, blocking collectives, per_device(): lax.all_to_all(outgoing(cotangent), 'seq', split_axis=0, concat_axis=0, t...  26.9 us
    all_to_all x1, blocking collectives, per_device(): lax.all_to_all(returning(total_v), 'seq', split_axis=0, concat_axis=0, ti...  20.6 us
    all_to_all x1, waiting for transfers between devices, per_device(): lax.all_to_all(outgoing(shared_qk), 'seq', split_axis=0, concat_axis=0, t...  16.8 us
    all_to_all x1, waiting for transfers between devices, per_device(): lax.all_to_all(returning(total_qk), 'seq', split_axis=0, concat_axis=0, t...  16.6 us
    all_to_all x1, waiting for transfers between devices, per_device(): lax.all_to_all(outgoing(values), 'seq', split_axis=0, concat_axis=0, tile...  13.8 us
    sub x4, matrix products, attend(): weight = jnp.where(allowed, jnp.exp(logit_scores - row_max), 0.0)  9.67 us
    dot_general x4, matrix products, attend(): jnp.einsum('ynp,ypm->ynm', probabilities_reduced, value_matrix_rows, pref...  9.32 us
    squeeze x24, local copies, waits for them, and re-layouts, run_attention(): lax.map(attend_items, tuple((split_turns(piece) for piece in pieces)))  8.02 us
  transfers between devices with their start and end apart: 3, of which 3 were waited for; matrix products, arithmetic and copies ran while one was open for 2% of the time, Pallas kernels for 0%

commit v1 on v0

v1 whole, which is shorter than its diff:
```python
import functools
import math

import jax
import jax.numpy as jnp
from jax import lax
from jax.experimental import pallas as pl
from jax.experimental.pallas import tpu as pltpu
from jax.sharding import PartitionSpec as P

BLOCK = 128
DH = 128
NT = (((1,), (1,)), ((), ()))
NN = (((1,), (0,)), ((), ()))
TN = (((0,), (0,)), ((), ()))


def dot(a, b, dims):
    return lax.dot_general(a, b, dims, preferred_element_type=jnp.float32)


def pack_kernel(per_source, group_size, ids_ref, a_ref, b_ref, c_ref, out_ref, sems):
    base = lax.axis_index("seq") * per_source
    copies = []
    for i in range(per_source):
        slot = ids_ref[base + i] // group_size
        for j, ref in enumerate((a_ref, b_ref, c_ref)):
            copy = pltpu.make_async_copy(
                ref.at[pl.ds(i * BLOCK, BLOCK)], out_ref.at[slot, j], sems.at[i, j]
            )
            copy.start()
            copies.append(copy)
    for copy in copies:
        copy.wait()


def unpack_kernel(per_source, group_size, ids_ref, in_ref, a_ref, b_ref, sems):
    base = lax.axis_index("seq") * per_source
    copies = []
    for i in range(per_source):
        slot = ids_ref[base + i] // group_size
        for j, ref in enumerate((a_ref, b_ref)):
            copy = pltpu.make_async_copy(
                in_ref.at[slot, j], ref.at[pl.ds(i * BLOCK, BLOCK)], sems.at[i, j]
            )
            copy.start()
            copies.append(copy)
    for copy in copies:
        copy.wait()


def attend_kernel(clusters, table_ref, in_ref, out_ref, carry_ref, first_ref):
    scale = 1.0 / math.sqrt(DH)
    factor = scale * math.log2(math.e)

    def attend(c, following, have_part, own_count, near_count):
        own_src = [table_ref[1 + p, c] for p in range(own_count)]
        near_src = [table_ref[1 + p, following] for p in range(near_count)]
        sources = own_src + near_src
        keys = [in_ref[s, 0] for s in sources]
        vals = [in_ref[s, 1] for s in sources]
        q = jnp.concatenate(keys[:own_count], axis=0)
        g = jnp.concatenate([in_ref[s, 2] for s in own_src], axis=0)
        width = own_count * BLOCK
        ahead = lax.broadcasted_iota(jnp.int32, (BLOCK, width), 1) - lax.broadcasted_iota(
            jnp.int32, (BLOCK, width), 0
        )
        scores = [dot(k, q, NT) for k in keys]
        for p in range(own_count):
            scores[p] = jnp.where(ahead == p * BLOCK, -1e30, scores[p])
        top = functools.reduce(jnp.maximum, [jnp.max(s, axis=0, keepdims=True) for s in scores])
        weights = [jnp.exp2((s - top) * factor) for s in scores]
        dprobs = [dot(v, g, NT) for v in vals]
        total = sum(jnp.sum(w, axis=0, keepdims=True) for w in weights)
        inverse = 1.0 / total
        delta = (
            sum(jnp.sum(w * d, axis=0, keepdims=True) for w, d in zip(weights, dprobs)) * inverse
        )
        probs = [w * inverse for w in weights]
        dscores = [(p * (d - delta)).astype(jnp.bfloat16) for p, d in zip(probs, dprobs)]
        grad_w = [dot(p.astype(jnp.bfloat16), g, NN) for p in probs]
        grad_k = [dot(s, q, NN) for s in dscores]
        grad_q = dot(
            jnp.concatenate(dscores, axis=0), jnp.concatenate(keys, axis=0), TN
        )
        for p in range(own_count):
            own_qk = (grad_q[p * BLOCK : (p + 1) * BLOCK] + grad_k[p]) * scale
            own_v = grad_w[p]
            own_qk = own_qk + jnp.where(have_part, carry_ref[0, p], 0.0)
            own_v = own_v + jnp.where(have_part, carry_ref[1, p], 0.0)
            out_ref[own_src[p], 0] = own_qk.astype(jnp.bfloat16)
            out_ref[own_src[p], 1] = own_v.astype(jnp.bfloat16)

            @pl.when(c == 0)
            def _():
                first_ref[0, p] = own_qk
                first_ref[1, p] = own_v

        for p in range(near_count):
            carry_ref[0, p] = grad_k[own_count + p] * scale
            carry_ref[1, p] = grad_w[own_count + p]

    def step(c, have_part):
        following = lax.rem(c + 1, clusters)
        own = table_ref[0, c]
        near = jnp.where(table_ref[3, c] > 0, table_ref[0, following], 0)
        for own_count in (1, 2):
            for near_count in (0, 1, 2):

                @pl.when((own == own_count) & (near == near_count))
                def _():
                    attend(c, following, have_part > 0, own_count, near_count)

        return ((own > 0) & (near > 0)).astype(jnp.int32)

    have_part = lax.fori_loop(0, clusters, step, jnp.int32(0))
    for p in range(2):

        @pl.when((have_part > 0) & (table_ref[0, 0] > p))
        def _():
            source = table_ref[1 + p, 0]
            for j in range(2):
                out_ref[source, j] = (first_ref[j, p] + carry_ref[j, p]).astype(jnp.bfloat16)


def per_device(shared_qk, values, cotangent, cluster_ids, neighbour):
    n_seq = lax.axis_size("seq")
    seq_index = lax.axis_index("seq")
    tokens, lanes = shared_qk.shape
    per_source = tokens // BLOCK
    group_size = neighbour.shape[0] // n_seq
    any_space = pl.BlockSpec(memory_space=pl.ANY)
    smem = pl.BlockSpec(memory_space=pltpu.SMEM)
    vmem = pl.BlockSpec(memory_space=pltpu.VMEM)

    sent = pl.pallas_call(
        functools.partial(pack_kernel, per_source, group_size),
        out_shape=jax.ShapeDtypeStruct((n_seq, 3, BLOCK, lanes), shared_qk.dtype),
        in_specs=[smem, any_space, any_space, any_space],
        out_specs=any_space,
        scratch_shapes=[pltpu.SemaphoreType.DMA((per_source, 3))],
        name="pack",
    )(cluster_ids, shared_qk, values, cotangent)
    arrived = lax.all_to_all(sent, "seq", split_axis=0, concat_axis=0, tiled=True)

    local = seq_index * group_size + jnp.arange(group_size, dtype=jnp.int32)
    member = cluster_ids[None, :] == local[:, None]
    source = jnp.arange(cluster_ids.shape[0], dtype=jnp.int32)[None, :] // per_source
    table = jnp.stack(
        [
            jnp.sum(member.astype(jnp.int32), axis=1),
            jnp.min(jnp.where(member, source, n_seq - 1), axis=1),
            jnp.max(jnp.where(member, source, 0), axis=1),
            lax.dynamic_slice_in_dim(neighbour, seq_index * group_size, group_size) + 1,
        ]
    )
    returned = pl.pallas_call(
        functools.partial(attend_kernel, group_size),
        out_shape=jax.ShapeDtypeStruct((n_seq, 2, BLOCK, lanes), shared_qk.dtype),
        in_specs=[smem, vmem],
        out_specs=vmem,
        scratch_shapes=[
            pltpu.VMEM((2, 2, BLOCK, lanes), jnp.float32),
            pltpu.VMEM((2, 2, BLOCK, lanes), jnp.float32),
        ],
        compiler_params=pltpu.CompilerParams(vmem_limit_bytes=32 * 1024 * 1024),
        name="attend",
    )(table, arrived)
    home = lax.all_to_all(returned, "seq", split_axis=0, concat_axis=0, tiled=True)

    out = jax.ShapeDtypeStruct((tokens, lanes), shared_qk.dtype)
    return pl.pallas_call(
        functools.partial(unpack_kernel, per_source, group_size),
        out_shape=(out, out),
        in_specs=[smem, any_space],
        out_specs=(any_space, any_space),
        scratch_shapes=[pltpu.SemaphoreType.DMA((per_source, 2))],
        name="unpack",
    )(cluster_ids, home)


def solution(mesh):
    in_specs = (P("seq", "head"), P("seq", "head"), P("seq", "head"), P(), P())
    out_specs = (P("seq", "head"), P("seq", "head"))
    return jax.shard_map(
        per_device, mesh=mesh, in_specs=in_specs, out_specs=out_specs, check_vma=False
    )
```

time: 187 us -> 178 us (0.952)
  Pallas kernels: 0 us -> 92.3 us
  local copies, waits for them, and re-layouts: 32.1 us -> 0.01 us
  matrix products: 30.5 us -> 0 us
  other arithmetic: 15 us -> 1 us
  blocking collectives: 47.6 us -> 34.6 us
  waiting for transfers between devices: 47.2 us -> 38.2 us
  starting transfers between devices: 12.6 us -> 10.6 us
    pallas_call x0 -> x3, Pallas kernels: none -> 92.3 us  [the longest x1 49.9 us: per_device(): pl.pallas_call(functools.partial(pack_kernel, per_source, group_size), ou...]
    dot_general x20 -> x0, matrix products: 20.8 us -> none  [the longest x4 9.32 us: attend(): jnp.einsum('ynp,ypm->ynm', probabilities_reduced, value_matrix_rows, pref...]
    all_to_all x2 -> x1, blocking collectives: 47.6 us -> 34.6 us  [per_device(): lax.all_to_all(returned, 'seq', split_axis=0, concat_axis=0, tiled=True)]
    gather x10 -> x0, local copies, waits for them, and re-layouts: 10.2 us -> none  [the longest x3 4.17 us: to_group_tiles(): return jnp.take(flat, tile_index, axis=0)]
    sub x4 -> x0, matrix products: 9.67 us -> none  [attend(): weight = jnp.where(allowed, jnp.exp(logit_scores - row_max), 0.0)]
    all_to_all x3 -> x1, waiting for transfers between devices: 47.2 us -> 38.2 us  [per_device(): lax.all_to_all(sent, 'seq', split_axis=0, concat_axis=0, tiled=True)]
    squeeze x24 -> x0, local copies, waits for them, and re-layouts: 8.02 us -> none  [run_attention(): lax.map(attend_items, tuple((split_turns(piece) for piece in pieces)))]
    reshape x2 -> x0, other arithmetic: 4.16 us -> none  [the longest x1 2.92 us: outgoing(): jnp.take(blocks, send_index, axis=0)]
  transfers between devices with their start and end apart: 3 -> 1, of which waited for: 3 -> 1; matrix products, arithmetic and copies ran while one was open for 2% -> 1% of each run, Pallas kernels for 0% -> 0%
where the time goes in v1:
time: 178 us
  Pallas kernels  92.3 us (52%)
  waiting for transfers between devices  38.2 us (21%)
  blocking collectives  34.6 us (19%)
  starting transfers between devices  10.6 us (6%)
    pallas_call x1, Pallas kernels, per_device(): pl.pallas_call(functools.partial(pack_kernel, per_source, group_size), ou...  49.9 us
    all_to_all x1, waiting for transfers between devices, per_device(): lax.all_to_all(sent, 'seq', split_axis=0, concat_axis=0, tiled=True)  38.2 us
    all_to_all x1, blocking collectives, per_device(): lax.all_to_all(returned, 'seq', split_axis=0, concat_axis=0, tiled=True)  34.6 us
    pallas_call x1, Pallas kernels, per_device(): pl.pallas_call(functools.partial(unpack_kernel, per_source, group_size),...  33.9 us
    all_to_all x1, starting transfers between devices, per_device(): lax.all_to_all(sent, 'seq', split_axis=0, concat_axis=0, tiled=True)  10.6 us
    pallas_call x1, Pallas kernels, per_device(): pl.pallas_call(functools.partial(attend_kernel, group_size), out_shape=ja...  8.6 us
  transfers between devices with their start and end apart: 1, of which 1 were waited for; matrix products, arithmetic and copies ran while one was open for 1% of the time, Pallas kernels for 0%

profile of v1, /device:TPU:1, one launch (start us, length us, event | category | flops | bytes accessed | tf_op | source)
XLA Modules:
  0.0 177.5 jit_solution(9416281643422541855)
XLA Ops:
  0.6 49.9 %pack.1 = bf16[32,3,128,128]{3,2,1,0:T(8,128)(2,1)} custom-call(s32[512]{0:T(512)} %ids_ref.3, bf16[2048,128]{1,0:T(8,128)(2,1)} %a_ref.1, bf16[2048,128]{1,0:T(8,128)(2,1)} %b_ref.1, bf16[2048,128]{1,0:T(8,128)(2,1)} %c_ref.1), custom_call_target="tpu_custom_call" | custom-call | tf_op jit(solution)/shard_map/pack/pallas_call | solution.py:136
  50.5 0.0 copy-start
  50.5 10.6 %all-to-all-start = ((bf16[32,3,128,128]{3,2,1,0:T(8,128)(2,1)}), bf16[32,3,128,128]{3,2,1,0:T(8,128)(2,1)S(1)}, u32[]{:S(2)}, u32[]{:S(2)}) async-start(bf16[32,3,128,128]{3,2,1,0:T(8,128)(2,1)} %pack.1), calls=%async_computation | async-start | bytes 6291456 | tf_op jit(solution)/shard_map/all_to_all | solution.py:144
  61.2 0.8 add_bitcast_fusion
  61.9 0.0 copy-done
  61.9 0.2 fusion.1
  62.2 38.2 %all-to-all-done.in_ref = bf16[32,3,128,128]{3,2,1,0:T(8,128)(2,1)S(1)} async-done(((bf16[32,3,128,128]{3,2,1,0:T(8,128)(2,1)}), bf16[32,3,128,128]{3,2,1,0:T(8,128)(2,1)S(1)}, u32[]{:S(2)}, u32[]{:S(2)}) %all-to-all-start) | async-done | bytes 3145760 | tf_op jit(solution)/shard_map/all_to_all | solution.py:144
  100.4 8.6 %attend.1 = bf16[32,2,128,128]{3,2,1,0:T(8,128)(2,1)S(1)} custom-call(s32[4,16]{1,0:T(4,128)S(1)} %pad_add_fusion.table_ref, bf16[32,3,128,128]{3,2,1,0:T(8,128)(2,1)S(1)} %all-to-all-done.in_ref), custom_call_target="tpu_custom_call" | custom-call | tf_op jit(solution)/shard_map/attend/pallas_call | solution.py:157
  109.0 34.6 %all_to_all.10.in_ref = bf16[32,2,128,128]{3,2,1,0:T(8,128)(2,1)} all-to-all(bf16[32,2,128,128]{3,2,1,0:T(8,128)(2,1)S(1)} %attend.1), channel_id=1, replica_groups=mesh['seq'=32,'head'=16] {'seq'}, dimensions={0} | all-to-all | bytes 4194304 | tf_op jit(solution)/shard_map/all_to_all | solution.py:169
  143.6 33.9 %unpack.1 = (bf16[2048,128]{1,0:T(8,128)(2,1)}, bf16[2048,128]{1,0:T(8,128)(2,1)}) custom-call(s32[512]{0:T(512)} %ids_ref.3, bf16[32,2,128,128]{3,2,1,0:T(8,128)(2,1)} %all_to_all.10.in_ref), custom_call_target="tpu_custom_call" | custom-call | tf_op jit(solution)/shard_map/unpack/pallas_call | solution.py:172
  (3 shorter events, 0.0 us)
Async XLA Ops:
  50.5 11.4 %copy-start = (s32[512]{0:T(512)S(1)}, s32[512]{0:T(512)}, u32[]{:S(2)}) copy-start(s32[512]{0:T(512)} %ids_ref.3) | copy-start | bytes 6148
  50.5 49.9 %all-to-all-start = ((bf16[32,3,128,128]{3,2,1,0:T(8,128)(2,1)}), bf16[32,3,128,128]{3,2,1,0:T(8,128)(2,1)S(1)}, u32[]{:S(2)}, u32[]{:S(2)}) async-start(bf16[32,3,128,128]{3,2,1,0:T(8,128)(2,1)} %pack.1), calls=%async_computation | async-start | bytes 6291456 | tf_op jit(solution)/shard_map/all_to_all | solution.py:144

commit v2 on v1

--- a/solution.py
+++ b/solution.py
@@ -137,7 +137,7 @@
         functools.partial(pack_kernel, per_source, group_size),
         out_shape=jax.ShapeDtypeStruct((n_seq, 3, BLOCK, lanes), shared_qk.dtype),
         in_specs=[smem, any_space, any_space, any_space],
-        out_specs=any_space,
+        out_specs=vmem,
         scratch_shapes=[pltpu.SemaphoreType.DMA((per_source, 3))],
         name="pack",
     )(cluster_ids, shared_qk, values, cotangent)
@@ -172,7 +172,7 @@
     return pl.pallas_call(
         functools.partial(unpack_kernel, per_source, group_size),
         out_shape=(out, out),
-        in_specs=[smem, any_space],
+        in_specs=[smem, vmem],
         out_specs=(any_space, any_space),
         scratch_shapes=[pltpu.SemaphoreType.DMA((per_source, 2))],
         name="unpack",

time: 178 us -> 101 us (0.57)
  Pallas kernels: 92.3 us -> 15.4 us
    pallas_call x1, Pallas kernels: 49.9 us -> 4.14 us  [per_device(): pl.pallas_call(functools.partial(pack_kernel, per_source, group_size), ou...]
    pallas_call x1, Pallas kernels: 33.9 us -> 2.85 us  [per_device(): pl.pallas_call(functools.partial(unpack_kernel, per_source, group_size),...]
where the time goes in v2:
time: 101 us; the launch traced here: 100 us
  waiting for transfers between devices  38.2 us (38%)
  blocking collectives  34.2 us (34%)
  Pallas kernels  15.4 us (15%)
  starting transfers between devices  10.6 us (10%)
    all_to_all x1, waiting for transfers between devices, per_device(): lax.all_to_all(sent, 'seq', split_axis=0, concat_axis=0, tiled=True)  38.2 us
    all_to_all x1, blocking collectives, per_device(): lax.all_to_all(returned, 'seq', split_axis=0, concat_axis=0, tiled=True)  34.2 us
    all_to_all x1, starting transfers between devices, per_device(): lax.all_to_all(sent, 'seq', split_axis=0, concat_axis=0, tiled=True)  10.6 us
    pallas_call x1, Pallas kernels, per_device(): pl.pallas_call(functools.partial(attend_kernel, group_size), out_shape=ja...  8.46 us
    pallas_call x1, Pallas kernels, per_device(): pl.pallas_call(functools.partial(pack_kernel, per_source, group_size), ou...  4.14 us
    pallas_call x1, Pallas kernels, per_device(): pl.pallas_call(functools.partial(unpack_kernel, per_source, group_size),...  2.85 us
  transfers between devices with their start and end apart: 1, of which 1 were waited for; matrix products, arithmetic and copies ran while one was open for 1% of the time, Pallas kernels for 0%

profile of v2, /device:TPU:1, one launch (start us, length us, event | category | flops | bytes accessed | tf_op | source)
XLA Modules:
  0.0 100.1 jit_solution(5916636812534087962)
XLA Ops:
  0.6 4.1 %pack.1 = bf16[32,3,128,128]{3,2,1,0:T(8,128)(2,1)} custom-call(s32[512]{0:T(512)} %ids_ref.3, bf16[2048,128]{1,0:T(8,128)(2,1)} %a_ref.1, bf16[2048,128]{1,0:T(8,128)(2,1)} %b_ref.1, bf16[2048,128]{1,0:T(8,128)(2,1)} %c_ref.1), custom_call_target="tpu_custom_call" | custom-call | tf_op jit(solution)/shard_map/pack/pallas_call | solution.py:136
  4.8 0.0 copy-start
  4.8 10.6 %all-to-all-start = ((bf16[32,3,128,128]{3,2,1,0:T(8,128)(2,1)}), bf16[32,3,128,128]{3,2,1,0:T(8,128)(2,1)S(1)}, u32[]{:S(2)}, u32[]{:S(2)}) async-start(bf16[32,3,128,128]{3,2,1,0:T(8,128)(2,1)} %pack.1), calls=%async_computation | async-start | bytes 6291456 | tf_op jit(solution)/shard_map/all_to_all | solution.py:144
  15.4 0.8 add_bitcast_fusion
  16.2 0.0 copy-done
  16.2 0.2 fusion.1
  16.4 38.2 %all-to-all-done.in_ref = bf16[32,3,128,128]{3,2,1,0:T(8,128)(2,1)S(1)} async-done(((bf16[32,3,128,128]{3,2,1,0:T(8,128)(2,1)}), bf16[32,3,128,128]{3,2,1,0:T(8,128)(2,1)S(1)}, u32[]{:S(2)}, u32[]{:S(2)}) %all-to-all-start) | async-done | bytes 3145760 | tf_op jit(solution)/shard_map/all_to_all | solution.py:144
  54.7 8.5 %attend.1 = bf16[32,2,128,128]{3,2,1,0:T(8,128)(2,1)S(1)} custom-call(s32[4,16]{1,0:T(4,128)S(1)} %pad_add_fusion.table_ref, bf16[32,3,128,128]{3,2,1,0:T(8,128)(2,1)S(1)} %all-to-all-done.in_ref), custom_call_target="tpu_custom_call" | custom-call | tf_op jit(solution)/shard_map/attend/pallas_call | solution.py:157
  63.1 34.2 %all_to_all.10.in_ref = bf16[32,2,128,128]{3,2,1,0:T(8,128)(2,1)} all-to-all(bf16[32,2,128,128]{3,2,1,0:T(8,128)(2,1)S(1)} %attend.1), channel_id=1, replica_groups=mesh['seq'=32,'head'=16] {'seq'}, dimensions={0} | all-to-all | bytes 4194304 | tf_op jit(solution)/shard_map/all_to_all | solution.py:169
  97.3 2.8 %unpack.1 = (bf16[2048,128]{1,0:T(8,128)(2,1)}, bf16[2048,128]{1,0:T(8,128)(2,1)}) custom-call(s32[512]{0:T(512)} %ids_ref.3, bf16[32,2,128,128]{3,2,1,0:T(8,128)(2,1)} %all_to_all.10.in_ref), custom_call_target="tpu_custom_call" | custom-call | tf_op jit(solution)/shard_map/unpack/pallas_call | solution.py:172
  (3 shorter events, 0.0 us)
Async XLA Ops:
  4.8 11.4 %copy-start = (s32[512]{0:T(512)S(1)}, s32[512]{0:T(512)}, u32[]{:S(2)}) copy-start(s32[512]{0:T(512)} %ids_ref.3) | copy-start | bytes 6148
  4.8 49.9 %all-to-all-start = ((bf16[32,3,128,128]{3,2,1,0:T(8,128)(2,1)}), bf16[32,3,128,128]{3,2,1,0:T(8,128)(2,1)S(1)}, u32[]{:S(2)}, u32[]{:S(2)}) async-start(bf16[32,3,128,128]{3,2,1,0:T(8,128)(2,1)} %pack.1), calls=%async_computation | async-start | bytes 6291456 | tf_op jit(solution)/shard_map/all_to_all | solution.py:144

commit v3 on v2

v3 whole, which is shorter than its diff:
```python
import functools
import math

import jax
import jax.numpy as jnp
from jax import lax
from jax.experimental import pallas as pl
from jax.experimental.pallas import tpu as pltpu
from jax.sharding import PartitionSpec as P

BLOCK = 128
DH = 128
NT = (((1,), (1,)), ((), ()))
NN = (((1,), (0,)), ((), ()))
TN = (((0,), (0,)), ((), ()))


def dot(a, b, dims):
    return lax.dot_general(a, b, dims, preferred_element_type=jnp.float32)


def blocks_of(rows):
    return [rows[i : i + BLOCK] for i in range(0, rows.shape[0], BLOCK)]


def pack_kernel(chunk, group_size, ids_ref, a_ref, b_ref, c_ref, out_ref, held, in_sems, out_sems):
    per_source = held.shape[0]
    base = lax.axis_index("seq") * per_source
    arriving, leaving = [], []
    for k in range(per_source // chunk):
        for j, ref in enumerate((a_ref, b_ref, c_ref)):
            blocks = pl.ds(k * chunk, chunk)
            copy = pltpu.make_async_copy(ref.at[blocks], held.at[blocks, j], in_sems.at[k, j])
            copy.start()
            arriving.append(copy)
    for k in range(per_source // chunk):
        for copy in arriving[3 * k : 3 * k + 3]:
            copy.wait()
        for i in range(k * chunk, (k + 1) * chunk):
            slot = lax.div(ids_ref[base + i], group_size)
            copy = pltpu.make_async_copy(held.at[i], out_ref.at[slot], out_sems.at[i])
            copy.start()
            leaving.append(copy)
    for copy in leaving:
        copy.wait()


def unpack_kernel(per_source, group_size, ids_ref, in_ref, a_ref, b_ref, sems):
    base = lax.axis_index("seq") * per_source
    copies = []
    for i in range(per_source):
        slot = ids_ref[base + i] // group_size
        for j, ref in enumerate((a_ref, b_ref)):
            copy = pltpu.make_async_copy(
                in_ref.at[slot, j], ref.at[pl.ds(i * BLOCK, BLOCK)], sems.at[i, j]
            )
            copy.start()
            copies.append(copy)
    for copy in copies:
        copy.wait()


def attend_kernel(clusters, lanes, table_ref, in_ref, out_ref, carry_ref, first_ref):
    scale = 1.0 / math.sqrt(DH)
    factor = scale * math.log2(math.e)
    length = clusters // lanes

    def following(c):
        return lax.rem(c + 1, clusters)

    def near_of(c):
        return jnp.where(table_ref[3, c] > 0, table_ref[0, following(c)], 0)

    def attend(c, have, lane, own_most, near_most):
        own, near = table_ref[0, c], near_of(c)
        own_src = [table_ref[1 + p, c] for p in range(own_most)]
        near_src = [table_ref[1 + p, following(c)] for p in range(near_most)]
        valid = [own > p for p in range(own_most)] + [near > p for p in range(near_most)]
        sources = own_src + near_src

        def load(which, p):
            block = in_ref[sources[p], which]
            return jnp.where(valid[p], block, jnp.zeros_like(block))

        count = own_most + near_most
        keys = [load(0, p) for p in range(count)]
        vals = [load(1, p) for p in range(count)]
        q = jnp.concatenate(keys[:own_most], axis=0)
        g = jnp.concatenate([load(2, p) for p in range(own_most)], axis=0)
        parts = [
            [jnp.where(have > p, carry_ref[lane, j, p], 0.0) for p in range(own_most)]
            for j in range(2)
        ]
        width = own_most * BLOCK
        ahead = lax.broadcasted_iota(jnp.int32, (BLOCK, width), 1) - lax.broadcasted_iota(
            jnp.int32, (BLOCK, width), 0
        )
        scores = blocks_of(dot(jnp.concatenate(keys, axis=0), q, NT))
        for p in range(count):
            if p < own_most:
                scores[p] = jnp.where(ahead == p * BLOCK, -1e30, scores[p])
            if p > 0:
                scores[p] = jnp.where(valid[p], scores[p], -1e30)
        top = functools.reduce(jnp.maximum, [jnp.max(s, axis=0, keepdims=True) for s in scores])
        weights = [jnp.exp2((s - top) * factor) for s in scores]
        dprobs = blocks_of(dot(jnp.concatenate(vals, axis=0), g, NT))
        total = sum(jnp.sum(w, axis=0, keepdims=True) for w in weights)
        inverse = 1.0 / total
        delta = (
            sum(jnp.sum(w * d, axis=0, keepdims=True) for w, d in zip(weights, dprobs)) * inverse
        )
        probs = [w * inverse for w in weights]
        dscores = [(p * (d - delta)).astype(jnp.bfloat16) for p, d in zip(probs, dprobs)]
        grad_w = blocks_of(dot(jnp.concatenate([p.astype(jnp.bfloat16) for p in probs], axis=0), g, NN))
        dscores = jnp.concatenate(dscores, axis=0)
        grad_k = blocks_of(dot(dscores, q, NN))
        grad_q = dot(dscores, jnp.concatenate(keys, axis=0), TN)
        own_grads = [
            (
                (grad_q[p * BLOCK : (p + 1) * BLOCK] + grad_k[p]) * scale + parts[0][p],
                grad_w[p] + parts[1][p],
            )
            for p in range(own_most)
        ]
        near_grads = [(grad_k[own_most + p] * scale, grad_w[own_most + p]) for p in range(near_most)]
        return own_src, own, own_grads, near_grads

    def attend_all(i, haves, own_most, near_most):
        results = [
            attend(i + lane * length, haves[lane], lane, own_most, near_most)
            for lane in range(lanes)
        ]
        for lane, (own_src, own, own_grads, near_grads) in enumerate(results):
            for p, grads in enumerate(near_grads):
                for j in range(2):
                    carry_ref[lane, j, p] = grads[j]
            for p, grads in enumerate(own_grads):

                @pl.when(own > p)
                def _():
                    for j in range(2):
                        out_ref[own_src[p], j] = grads[j].astype(jnp.bfloat16)

                @pl.when(i == 0)
                def _():
                    for j in range(2):
                        first_ref[lane, j, p] = grads[j]

    def step(i, haves):
        cs = [i + lane * length for lane in range(lanes)]
        owns = [table_ref[0, c] for c in cs]
        nears = [jnp.where(own > 0, near_of(c), 0) for own, c in zip(owns, cs)]
        own_top = functools.reduce(jnp.maximum, owns)
        near_top = functools.reduce(jnp.maximum, nears)
        for own_most in (1, 2):
            for near_most in (0, 1, 2):

                @pl.when((own_top == own_most) & (near_top == near_most))
                def _():
                    attend_all(i, haves, own_most, near_most)

        return tuple(nears)

    haves = lax.fori_loop(0, length, step, (jnp.int32(0),) * lanes)
    for lane in range(lanes):
        c = lane * length
        for p in range(2):

            @pl.when((haves[lane - 1] > p) & (table_ref[0, c] > p))
            def _():
                source = table_ref[1 + p, c]
                for j in range(2):
                    total = first_ref[lane, j, p] + carry_ref[(lane - 1) % lanes, j, p]
                    out_ref[source, j] = total.astype(jnp.bfloat16)


def per_device(shared_qk, values, cotangent, cluster_ids, neighbour):
    n_seq = lax.axis_size("seq")
    seq_index = lax.axis_index("seq")
    tokens, lanes = shared_qk.shape
    per_source = tokens // BLOCK
    group_size = neighbour.shape[0] // n_seq
    any_space = pl.BlockSpec(memory_space=pl.ANY)
    smem = pl.BlockSpec(memory_space=pltpu.SMEM)
    vmem = pl.BlockSpec(memory_space=pltpu.VMEM)

    sent = pl.pallas_call(
        functools.partial(pack_kernel, 4, group_size),
        out_shape=jax.ShapeDtypeStruct((n_seq, 3, BLOCK, lanes), shared_qk.dtype),
        in_specs=[smem, any_space, any_space, any_space],
        out_specs=any_space,
        scratch_shapes=[
            pltpu.VMEM((per_source, 3, BLOCK, lanes), shared_qk.dtype),
            pltpu.SemaphoreType.DMA((per_source // 4, 3)),
            pltpu.SemaphoreType.DMA((per_source,)),
        ],
        name="pack",
    )(cluster_ids, *(x.reshape(-1, BLOCK, lanes) for x in (shared_qk, values, cotangent)))
    arrived = lax.all_to_all(sent, "seq", split_axis=0, concat_axis=0, tiled=True)

    local = seq_index * group_size + jnp.arange(group_size, dtype=jnp.int32)
    member = cluster_ids[None, :] == local[:, None]
    source = jnp.arange(cluster_ids.shape[0], dtype=jnp.int32)[None, :] // per_source
    table = jnp.stack(
        [
            jnp.sum(member.astype(jnp.int32), axis=1),
            jnp.min(jnp.where(member, source, n_seq - 1), axis=1),
            jnp.max(jnp.where(member, source, 0), axis=1),
            lax.dynamic_slice_in_dim(neighbour, seq_index * group_size, group_size) + 1,
        ]
    )
    returned = pl.pallas_call(
        functools.partial(attend_kernel, group_size, 1),
        out_shape=jax.ShapeDtypeStruct((n_seq, 2, BLOCK, lanes), shared_qk.dtype),
        in_specs=[smem, vmem],
        out_specs=vmem,
        scratch_shapes=[
            pltpu.VMEM((2, 2, 2, BLOCK, lanes), jnp.float32),
            pltpu.VMEM((2, 2, 2, BLOCK, lanes), jnp.float32),
        ],
        compiler_params=pltpu.CompilerParams(vmem_limit_bytes=16 * 1024 * 1024),
        name="attend",
    )(table, arrived)
    home = lax.all_to_all(returned, "seq", split_axis=0, concat_axis=0, tiled=True)

    out = jax.ShapeDtypeStruct((tokens, lanes), shared_qk.dtype)
    return pl.pallas_call(
        functools.partial(unpack_kernel, per_source, group_size),
        out_shape=(out, out),
        in_specs=[smem, vmem],
        out_specs=(any_space, any_space),
        scratch_shapes=[pltpu.SemaphoreType.DMA((per_source, 2))],
        compiler_params=pltpu.CompilerParams(vmem_limit_bytes=8 * 1024 * 1024),
        name="unpack",
    )(cluster_ids, home)


def solution(mesh):
    in_specs = (P("seq", "head"), P("seq", "head"), P("seq", "head"), P(), P())
    out_specs = (P("seq", "head"), P("seq", "head"))
    return jax.shard_map(
        per_device, mesh=mesh, in_specs=in_specs, out_specs=out_specs, check_vma=False
    )
```

time: 101 us -> 97.6 us (0.966)
  Pallas kernels: 15.4 us -> 13.1 us
    pallas_call x2, Pallas kernels: 12.6 us -> 11.3 us  [the longest x1 8.17 us: per_device(): pl.pallas_call(functools.partial(attend_kernel, group_size, 1), out_shape...]
    pallas_call x1, Pallas kernels: 2.85 us -> 1.81 us  [per_device(): pl.pallas_call(functools.partial(unpack_kernel, per_source, group_size),...]
where the time goes in v3:
time: 97.6 us; the launch traced here: 97.3 us
  waiting for transfers between devices  38.2 us (39%)
  blocking collectives  33.7 us (35%)
  Pallas kernels  13.1 us (13%)
  starting transfers between devices  10.6 us (11%)
  other arithmetic  1 us (1%)
    all_to_all x1, waiting for transfers between devices, per_device(): lax.all_to_all(sent, 'seq', split_axis=0, concat_axis=0, tiled=True)  38.2 us
    all_to_all x1, blocking collectives, per_device(): lax.all_to_all(returned, 'seq', split_axis=0, concat_axis=0, tiled=True)  33.7 us
    all_to_all x1, starting transfers between devices, per_device(): lax.all_to_all(sent, 'seq', split_axis=0, concat_axis=0, tiled=True)  10.6 us
    pallas_call x1, Pallas kernels, per_device(): pl.pallas_call(functools.partial(attend_kernel, group_size, 1), out_shape...  8.17 us
    pallas_call x1, Pallas kernels, per_device(): pl.pallas_call(functools.partial(pack_kernel, 4, group_size), out_shape=j...  3.14 us
  transfers between devices with their start and end apart: 1, of which 1 were waited for; matrix products, arithmetic and copies ran while one was open for 1% of the time, Pallas kernels for 0%

profile of v3, /device:TPU:1, one launch (start us, length us, event | category | flops | bytes accessed | tf_op | source)
XLA Modules:
  0.0 97.3 jit_solution(4828544676248572588)
XLA Ops:
  0.6 3.1 %pack.1 = bf16[32,3,128,128]{3,2,1,0:T(8,128)(2,1)} custom-call(s32[512]{0:T(512)} %ids_ref.3, bf16[16,128,128]{2,1,0:T(8,128)(2,1)} %bitcast.8, bf16[16,128,128]{2,1,0:T(8,128)(2,1)} %bitcast.9, bf16[16,128,128]{2,1,0:T(8,128)(2,1)} %bitcast.10), custom_call_target="tpu_custom_call" | custom-call | tf_op jit(solution)/shard_map/pack/pallas_call | solution.py:187
  3.8 0.0 copy-start
  3.8 10.6 %all-to-all-start = ((bf16[32,3,128,128]{3,2,1,0:T(8,128)(2,1)}), bf16[32,3,128,128]{3,2,1,0:T(8,128)(2,1)S(1)}, u32[]{:S(2)}, u32[]{:S(2)}) async-start(bf16[32,3,128,128]{3,2,1,0:T(8,128)(2,1)} %pack.1), calls=%async_computation | async-start | bytes 6291456 | tf_op jit(solution)/shard_map/all_to_all | solution.py:199
  14.4 0.8 add_bitcast_fusion
  15.2 0.0 copy-done
  15.2 0.2 fusion.1
  15.4 38.2 %all-to-all-done.in_ref = bf16[32,3,128,128]{3,2,1,0:T(8,128)(2,1)S(1)} async-done(((bf16[32,3,128,128]{3,2,1,0:T(8,128)(2,1)}), bf16[32,3,128,128]{3,2,1,0:T(8,128)(2,1)S(1)}, u32[]{:S(2)}, u32[]{:S(2)}) %all-to-all-start) | async-done | bytes 3145760 | tf_op jit(solution)/shard_map/all_to_all | solution.py:199
  53.7 8.2 %attend.1 = bf16[32,2,128,128]{3,2,1,0:T(8,128)(2,1)S(1)} custom-call(s32[4,16]{1,0:T(4,128)S(1)} %pad_add_fusion.table_ref, bf16[32,3,128,128]{3,2,1,0:T(8,128)(2,1)S(1)} %all-to-all-done.in_ref), custom_call_target="tpu_custom_call" | custom-call | tf_op jit(solution)/shard_map/attend/pallas_call | solution.py:212
  61.9 33.7 %all_to_all.10.in_ref = bf16[32,2,128,128]{3,2,1,0:T(8,128)(2,1)S(1)} all-to-all(bf16[32,2,128,128]{3,2,1,0:T(8,128)(2,1)S(1)} %attend.1), channel_id=1, replica_groups=mesh['seq'=32,'head'=16] {'seq'}, dimensions={0} | all-to-all | bytes 4194304 | tf_op jit(solution)/shard_map/all_to_all | solution.py:224
  95.5 1.8 %unpack.1 = (bf16[2048,128]{1,0:T(8,128)(2,1)}, bf16[2048,128]{1,0:T(8,128)(2,1)}) custom-call(s32[512]{0:T(512)S(1)} %copy-done, bf16[32,2,128,128]{3,2,1,0:T(8,128)(2,1)S(1)} %all_to_all.10.in_ref), custom_call_target="tpu_custom_call" | custom-call | tf_op jit(solution)/shard_map/unpack/pallas_call | solution.py:227
  (3 shorter events, 0.0 us)
Async XLA Ops:
  3.8 11.4 %copy-start = (s32[512]{0:T(512)S(1)}, s32[512]{0:T(512)}, u32[]{:S(2)}) copy-start(s32[512]{0:T(512)} %ids_ref.3) | copy-start | bytes 6148
  3.8 49.9 %all-to-all-start = ((bf16[32,3,128,128]{3,2,1,0:T(8,128)(2,1)}), bf16[32,3,128,128]{3,2,1,0:T(8,128)(2,1)S(1)}, u32[]{:S(2)}, u32[]{:S(2)}) async-start(bf16[32,3,128,128]{3,2,1,0:T(8,128)(2,1)} %pack.1), calls=%async_computation | async-start | bytes 6291456 | tf_op jit(solution)/shard_map/all_to_all | solution.py:199

commit v4 on v2

v4 whole, which is shorter than its diff:
```python
import functools
import math

import jax
import jax.numpy as jnp
from jax import lax
from jax.experimental import pallas as pl
from jax.experimental.pallas import tpu as pltpu
from jax.sharding import PartitionSpec as P

BLOCK = 128
DH = 128
TOGETHER = (4, 4, 2, 2, 2, 2)
NT = (((1,), (1,)), ((), ()))
NN = (((1,), (0,)), ((), ()))
TN = (((0,), (0,)), ((), ()))


def dot(a, b, dims):
    return lax.dot_general(a, b, dims, preferred_element_type=jnp.float32)


def pack_kernel(chunk, group_size, ids_ref, a_ref, b_ref, c_ref, out_ref, held, in_sems, out_sems):
    per_source = held.shape[0]
    base = lax.axis_index("seq") * per_source
    arriving, leaving = [], []
    for k in range(per_source // chunk):
        for j, ref in enumerate((a_ref, b_ref, c_ref)):
            blocks = pl.ds(k * chunk, chunk)
            copy = pltpu.make_async_copy(ref.at[blocks], held.at[blocks, j], in_sems.at[k, j])
            copy.start()
            arriving.append(copy)
    for k in range(per_source // chunk):
        for copy in arriving[3 * k : 3 * k + 3]:
            copy.wait()
        for i in range(k * chunk, (k + 1) * chunk):
            slot = lax.div(ids_ref[base + i], group_size)
            copy = pltpu.make_async_copy(held.at[i], out_ref.at[slot], out_sems.at[i])
            copy.start()
            leaving.append(copy)
    for copy in leaving:
        copy.wait()


def unpack_kernel(per_source, group_size, ids_ref, in_ref, a_ref, b_ref, sems):
    base = lax.axis_index("seq") * per_source
    copies = []
    for i in range(per_source):
        slot = ids_ref[base + i] // group_size
        for j, ref in enumerate((a_ref, b_ref)):
            copy = pltpu.make_async_copy(
                in_ref.at[slot, j], ref.at[pl.ds(i * BLOCK, BLOCK)], sems.at[i, j]
            )
            copy.start()
            copies.append(copy)
    for copy in copies:
        copy.wait()


def attend_kernel(clusters, together, table_ref, in_ref, out_ref, own_ref, part_ref):
    scale = 1.0 / math.sqrt(DH)
    factor = scale * math.log2(math.e)

    def attend(cs, own_count, near_count):
        lanes = range(len(cs))
        own_src = [[table_ref[1 + p, c] for p in range(own_count)] for c in cs]
        near_src = [
            [table_ref[1 + p, lax.rem(c + 1, clusters)] for p in range(near_count)] for c in cs
        ]

        def load(which, sources):
            return jnp.concatenate([in_ref[s, which] for s in sources], axis=0)

        k = [load(0, own_src[i] + near_src[i]) for i in lanes]
        w = [load(1, own_src[i] + near_src[i]) for i in lanes]
        g = [load(2, own_src[i]) for i in lanes]
        width = own_count * BLOCK
        q = [x[:width] for x in k]
        ahead = lax.broadcasted_iota(jnp.int32, (width, width), 1) - lax.broadcasted_iota(
            jnp.int32, (width, width), 0
        )
        scores = [dot(k[i], q[i], NT) for i in lanes]
        dprobs = [dot(w[i], g[i], NT) for i in lanes]
        own_scores = [jnp.where(ahead == 0, -1e30, x[:width]) for x in scores]
        if near_count:
            scores = [jnp.concatenate([own_scores[i], scores[i][width:]], axis=0) for i in lanes]
        else:
            scores = own_scores
        top = [jnp.max(x, axis=0, keepdims=True) for x in scores]
        weights = [jnp.exp2((scores[i] - top[i]) * factor) for i in lanes]
        inverse = [1.0 / jnp.sum(x, axis=0, keepdims=True) for x in weights]
        delta = [
            jnp.sum(weights[i] * dprobs[i], axis=0, keepdims=True) * inverse[i] for i in lanes
        ]
        probs = [weights[i] * inverse[i] for i in lanes]
        dscores = [(probs[i] * (dprobs[i] - delta[i])).astype(jnp.bfloat16) for i in lanes]
        grad_q = [dot(dscores[i], k[i], TN) for i in lanes]
        grad_w = [dot(probs[i].astype(jnp.bfloat16), g[i], NN) for i in lanes]
        grad_k = [dot(dscores[i], q[i], NN) for i in lanes]
        for i in lanes:
            for p in range(own_count):
                rows = slice(p * BLOCK, (p + 1) * BLOCK)
                own_ref[0, own_src[i][p]] = (grad_q[i][rows] + grad_k[i][rows]) * scale
                own_ref[1, own_src[i][p]] = grad_w[i][rows]
            for p in range(near_count):
                rows = slice(width + p * BLOCK, width + (p + 1) * BLOCK)
                part_ref[0, near_src[i][p]] = grad_k[i][rows] * scale
                part_ref[1, near_src[i][p]] = grad_w[i][rows]

    for own_count in (1, 2):
        for near_count in (0, 1, 2):
            shape = 3 * own_count + near_count
            first, end = table_ref[6, shape], table_ref[6, shape + 1]
            lanes = together[shape - 3]

            @pl.loop(0, lax.div(end - first + (lanes - 1), lanes))
            def _(turn):
                at = [jnp.minimum(first + turn * lanes + i, end - 1) for i in range(lanes)]
                attend([table_ref[5, a] for a in at], own_count, near_count)

    @pl.loop(0, clusters, unroll=True)
    def _(c):
        for p in range(2):
            source = table_ref[1 + p, c]

            @pl.when(table_ref[0, c] > p)
            def _():
                for j in range(2):
                    part = jnp.where(table_ref[4, c] > p, part_ref[j, source], 0.0)
                    out_ref[source, j] = (own_ref[j, source] + part).astype(jnp.bfloat16)


def per_device(shared_qk, values, cotangent, cluster_ids, neighbour):
    n_seq = lax.axis_size("seq")
    seq_index = lax.axis_index("seq")
    tokens, lanes = shared_qk.shape
    per_source = tokens // BLOCK
    group_size = neighbour.shape[0] // n_seq
    any_space = pl.BlockSpec(memory_space=pl.ANY)
    smem = pl.BlockSpec(memory_space=pltpu.SMEM)
    vmem = pl.BlockSpec(memory_space=pltpu.VMEM)

    sent = pl.pallas_call(
        functools.partial(pack_kernel, 4, group_size),
        out_shape=jax.ShapeDtypeStruct((n_seq, 3, BLOCK, lanes), shared_qk.dtype),
        in_specs=[smem, any_space, any_space, any_space],
        out_specs=any_space,
        scratch_shapes=[
            pltpu.VMEM((per_source, 3, BLOCK, lanes), shared_qk.dtype),
            pltpu.SemaphoreType.DMA((per_source // 4, 3)),
            pltpu.SemaphoreType.DMA((per_source,)),
        ],
        name="pack",
    )(cluster_ids, *(x.reshape(-1, BLOCK, lanes) for x in (shared_qk, values, cotangent)))
    arrived = lax.all_to_all(sent, "seq", split_axis=0, concat_axis=0, tiled=True)

    local = seq_index * group_size + jnp.arange(group_size, dtype=jnp.int32)
    member = cluster_ids[None, :] == local[:, None]
    source = jnp.arange(cluster_ids.shape[0], dtype=jnp.int32)[None, :] // per_source
    held = jnp.sum(member.astype(jnp.int32), axis=1)
    flagged = lax.dynamic_slice_in_dim(neighbour, seq_index * group_size, group_size) >= 0
    near = jnp.where(flagged & (held > 0), jnp.roll(held, -1), 0)
    shape = 3 * held + near
    ids = jnp.arange(group_size, dtype=jnp.int32)
    before = (shape[None, :] < shape[:, None]) | (
        (shape[None, :] == shape[:, None]) & (ids[None, :] < ids[:, None])
    )
    rank = jnp.sum(before.astype(jnp.int32), axis=1)
    order = jnp.sum(jnp.where(rank[None, :] == ids[:, None], ids[None, :], 0), axis=1)
    starts = jnp.sum((shape[None, :] < ids[:, None]).astype(jnp.int32), axis=1)
    table = jnp.stack(
        [
            held,
            jnp.min(jnp.where(member, source, n_seq - 1), axis=1),
            jnp.max(jnp.where(member, source, 0), axis=1),
            near,
            jnp.roll(near, 1),
            order,
            starts,
        ]
    )
    returned = pl.pallas_call(
        functools.partial(attend_kernel, group_size, TOGETHER),
        out_shape=jax.ShapeDtypeStruct((n_seq, 2, BLOCK, lanes), shared_qk.dtype),
        in_specs=[smem, vmem],
        out_specs=vmem,
        scratch_shapes=[
            pltpu.VMEM((2, n_seq, BLOCK, lanes), jnp.float32),
            pltpu.VMEM((2, n_seq, BLOCK, lanes), jnp.float32),
        ],
        compiler_params=pltpu.CompilerParams(vmem_limit_bytes=32 * 1024 * 1024),
        name="attend",
    )(table, arrived)
    home = lax.all_to_all(returned, "seq", split_axis=0, concat_axis=0, tiled=True)

    out = jax.ShapeDtypeStruct((tokens, lanes), shared_qk.dtype)
    return pl.pallas_call(
        functools.partial(unpack_kernel, per_source, group_size),
        out_shape=(out, out),
        in_specs=[smem, vmem],
        out_specs=(any_space, any_space),
        scratch_shapes=[pltpu.SemaphoreType.DMA((per_source, 2))],
        compiler_params=pltpu.CompilerParams(vmem_limit_bytes=8 * 1024 * 1024),
        name="unpack",
    )(cluster_ids, home)


def solution(mesh):
    in_specs = (P("seq", "head"), P("seq", "head"), P("seq", "head"), P(), P())
    out_specs = (P("seq", "head"), P("seq", "head"))
    return jax.shard_map(
        per_device, mesh=mesh, in_specs=in_specs, out_specs=out_specs, check_vma=False
    )
```

time: 101 us -> 95.3 us (0.944)
  Pallas kernels: 15.4 us -> 11.2 us
  waiting for transfers between devices: 38.2 us -> 36.5 us
  other arithmetic: 1 us -> 2.04 us
    pallas_call x2, Pallas kernels: 12.6 us -> 9.4 us  [the longest x1 6.26 us: per_device(): pl.pallas_call(functools.partial(attend_kernel, group_size, TOGETHER), ou...]
    all_to_all x1, waiting for transfers between devices: 38.2 us -> 36.5 us  [per_device(): lax.all_to_all(sent, 'seq', split_axis=0, concat_axis=0, tiled=True)]
    pallas_call x1, Pallas kernels: 2.85 us -> 1.81 us  [per_device(): pl.pallas_call(functools.partial(unpack_kernel, per_source, group_size),...]
  transfers between devices with their start and end apart: 1 -> 1, of which waited for: 1 -> 1; matrix products, arithmetic and copies ran while one was open for 1% -> 3% of each run, Pallas kernels for 0% -> 0%
where the time goes in v4:
time: 95.3 us; the launch traced here: 95 us
  waiting for transfers between devices  36.5 us (38%)
  blocking collectives  33.3 us (35%)
  Pallas kernels  11.2 us (12%)
  starting transfers between devices  10.6 us (11%)
  other arithmetic  2.04 us (2%)
    all_to_all x1, waiting for transfers between devices, per_device(): lax.all_to_all(sent, 'seq', split_axis=0, concat_axis=0, tiled=True)  36.5 us
    all_to_all x1, blocking collectives, per_device(): lax.all_to_all(returned, 'seq', split_axis=0, concat_axis=0, tiled=True)  33.3 us
    all_to_all x1, starting transfers between devices, per_device(): lax.all_to_all(sent, 'seq', split_axis=0, concat_axis=0, tiled=True)  10.6 us
    pallas_call x1, Pallas kernels, per_device(): pl.pallas_call(functools.partial(attend_kernel, group_size, TOGETHER), ou...  6.26 us
    pallas_call x1, Pallas kernels, per_device(): pl.pallas_call(functools.partial(pack_kernel, 4, group_size), out_shape=j...  3.14 us
  transfers between devices with their start and end apart: 1, of which 1 were waited for; matrix products, arithmetic and copies ran while one was open for 3% of the time, Pallas kernels for 0%

profile of v4, /device:TPU:1, one launch (start us, length us, event | category | flops | bytes accessed | tf_op | source)
XLA Modules:
  0.0 95.0 jit_solution(13232988888970759778)
XLA Ops:
  0.6 3.1 %pack.1 = bf16[32,3,128,128]{3,2,1,0:T(8,128)(2,1)} custom-call(s32[512]{0:T(512)} %ids_ref.3, bf16[16,128,128]{2,1,0:T(8,128)(2,1)} %bitcast.13, bf16[16,128,128]{2,1,0:T(8,128)(2,1)} %bitcast.14, bf16[16,128,128]{2,1,0:T(8,128)(2,1)} %bitcast.15), custom_call_target="tpu_custom_call" | custom-call | tf_op jit(solution)/shard_map/pack/pallas_call | solution.py:143
  3.8 0.0 copy-start
  3.8 10.6 %all-to-all-start = ((bf16[32,3,128,128]{3,2,1,0:T(8,128)(2,1)}), bf16[32,3,128,128]{3,2,1,0:T(8,128)(2,1)S(1)}, u32[]{:S(2)}, u32[]{:S(2)}) async-start(bf16[32,3,128,128]{3,2,1,0:T(8,128)(2,1)} %pack.1), calls=%async_computation | async-start | bytes 6291456 | tf_op jit(solution)/shard_map/all_to_all | solution.py:155
  14.4 0.0 copy-done
  14.5 0.2 fusion.2
  14.7 0.1 slice.16
  14.8 0.8 multiply_add_fusion
  15.6 0.6 slice.18
  16.1 0.7 add_bitcast_fusion
  16.9 0.2 convert_reduce_fusion
  17.0 0.1 select_reduce_fusion
  17.2 36.5 %all-to-all-done.in_ref = bf16[32,3,128,128]{3,2,1,0:T(8,128)(2,1)S(1)} async-done(((bf16[32,3,128,128]{3,2,1,0:T(8,128)(2,1)}), bf16[32,3,128,128]{3,2,1,0:T(8,128)(2,1)S(1)}, u32[]{:S(2)}, u32[]{:S(2)}) %all-to-all-start) | async-done | bytes 3145760 | tf_op jit(solution)/shard_map/all_to_all | solution.py:155
  53.7 6.3 %attend.1 = bf16[32,2,128,128]{3,2,1,0:T(8,128)(2,1)S(1)} custom-call(s32[7,16]{1,0:T(8,128)S(1)} %stack.31.table_ref, bf16[32,3,128,128]{3,2,1,0:T(8,128)(2,1)S(1)} %all-to-all-done.in_ref), custom_call_target="tpu_custom_call" | custom-call | tf_op jit(solution)/shard_map/attend/pallas_call | solution.py:182
  60.0 33.3 %all_to_all.10.in_ref = bf16[32,2,128,128]{3,2,1,0:T(8,128)(2,1)S(1)} all-to-all(bf16[32,2,128,128]{3,2,1,0:T(8,128)(2,1)S(1)} %attend.1), channel_id=1, replica_groups=mesh['seq'=32,'head'=16] {'seq'}, dimensions={0} | all-to-all | bytes 4194304 | tf_op jit(solution)/shard_map/all_to_all | solution.py:194
  93.2 1.8 %unpack.1 = (bf16[2048,128]{1,0:T(8,128)(2,1)}, bf16[2048,128]{1,0:T(8,128)(2,1)}) custom-call(s32[512]{0:T(512)S(1)} %copy-done, bf16[32,2,128,128]{3,2,1,0:T(8,128)(2,1)S(1)} %all_to_all.10.in_ref), custom_call_target="tpu_custom_call" | custom-call | tf_op jit(solution)/shard_map/unpack/pallas_call | solution.py:197
  (3 shorter events, 0.0 us)
Async XLA Ops:
  3.8 10.7 %copy-start = (s32[512]{0:T(512)S(1)}, s32[512]{0:T(512)}, u32[]{:S(2)}) copy-start(s32[512]{0:T(512)} %ids_ref.3) | copy-start | bytes 6148
  3.8 49.9 %all-to-all-start = ((bf16[32,3,128,128]{3,2,1,0:T(8,128)(2,1)}), bf16[32,3,128,128]{3,2,1,0:T(8,128)(2,1)S(1)}, u32[]{:S(2)}, u32[]{:S(2)}) async-start(bf16[32,3,128,128]{3,2,1,0:T(8,128)(2,1)} %pack.1), calls=%async_computation | async-start | bytes 6291456 | tf_op jit(solution)/shard_map/all_to_all | solution.py:155

commit v5 on v4

v5 whole, which is shorter than its diff:
```python
import functools
import math

import jax
import jax.numpy as jnp
from jax import lax
from jax.experimental import pallas as pl
from jax.experimental.pallas import tpu as pltpu
from jax.sharding import PartitionSpec as P

BLOCK = 128
DH = 128
TOGETHER = (4, 4, 2, 2, 2, 2)
PACK, UNPACK = 8, 8
NT = (((1,), (1,)), ((), ()))
NN = (((1,), (0,)), ((), ()))
TN = (((0,), (0,)), ((), ()))


def dot(a, b, dims):
    return lax.dot_general(a, b, dims, preferred_element_type=jnp.float32)


def make_table(ids, neighbour, group_size, per_source, n_seq, table_ref):
    total = ids.shape[1]
    member_of = lax.broadcasted_iota(jnp.int32, (group_size, total), 0)
    local = member_of + lax.axis_index("seq") * group_size
    lane = lax.broadcasted_iota(jnp.int32, (group_size, total), 1)
    member = ids == local
    source = lax.div(lane, per_source)

    def count(mask):
        return jnp.sum(jnp.where(mask, 1, 0), axis=1, keepdims=True)

    held = count(member)
    low = jnp.min(jnp.where(member, source, n_seq - 1), axis=1, keepdims=True)
    high = jnp.max(jnp.where(member, source, 0), axis=1, keepdims=True)
    flagged = count((lane == local) & (neighbour >= 0))
    i = lax.broadcasted_iota(jnp.int32, (group_size, group_size), 0)
    j = lax.broadcasted_iota(jnp.int32, (group_size, group_size), 1)

    def as_row(column):
        return jnp.sum(jnp.where(i == j, column, 0), axis=0, keepdims=True)

    def picked(row, mask):
        return jnp.sum(jnp.where(mask, row, 0), axis=1, keepdims=True)

    following = picked(as_row(held), j == lax.rem(i + 1, group_size))
    near = jnp.where((flagged > 0) & (held > 0), following, 0)
    part = picked(as_row(near), j == lax.rem(i + (group_size - 1), group_size))
    shape = 3 * held + near
    shape_row = as_row(shape)
    rank = count((shape_row < shape) | ((shape_row == shape) & (j < i)))
    order = picked(j, as_row(rank) == i)
    starts = count(shape_row < i)
    place = lax.broadcasted_iota(jnp.int32, table_ref.shape, 1)
    table = jnp.zeros(table_ref.shape, jnp.int32)
    for k, column in enumerate((held, low, high, near, part, order, starts)):
        table = jnp.where(place == k, column, table)
    table_ref[...] = table


def pack_kernel(
    chunk,
    group_size,
    ids_ref,
    row_ref,
    near_ref,
    a_ref,
    b_ref,
    c_ref,
    out_ref,
    table_ref,
    ids,
    row,
    near,
    table,
    held,
    small_sems,
    in_sems,
    out_sems,
):
    per_source = held.shape[0]
    base = lax.axis_index("seq") * per_source
    small = [
        pltpu.make_async_copy(ref, scratch, small_sems.at[k])
        for k, (ref, scratch) in enumerate(((ids_ref, ids), (row_ref, row), (near_ref, near)))
    ]
    for copy in small:
        copy.start()
    arriving, leaving = [], []
    for k in range(per_source // chunk):
        for j, ref in enumerate((a_ref, b_ref, c_ref)):
            blocks = pl.ds(k * chunk, chunk)
            copy = pltpu.make_async_copy(ref.at[blocks], held.at[blocks, j], in_sems.at[k, j])
            copy.start()
            arriving.append(copy)
    for copy in small:
        copy.wait()
    slots = [lax.div(ids[base + i], group_size) for i in range(per_source)]
    for k in range(per_source // chunk):
        for copy in arriving[3 * k : 3 * k + 3]:
            copy.wait()
        for i in range(k * chunk, (k + 1) * chunk):
            copy = pltpu.make_async_copy(held.at[i], out_ref.at[slots[i]], out_sems.at[i])
            copy.start()
            leaving.append(copy)
    make_table(row[...], near[...], group_size, per_source, out_ref.shape[0], table)
    tabled = pltpu.make_async_copy(table, table_ref, small_sems.at[3])
    tabled.start()
    tabled.wait()
    for copy in leaving:
        copy.wait()


def unpack_kernel(chunk, group_size, ids_ref, in_ref, a_ref, b_ref, held, sems):
    per_source = held.shape[1]
    base = lax.axis_index("seq") * per_source
    leaving = []
    for k in range(per_source // chunk):
        for j, ref in enumerate((a_ref, b_ref)):
            for i in range(k * chunk, (k + 1) * chunk):
                held[j, i] = in_ref[lax.div(ids_ref[base + i], group_size), j]
            blocks = pl.ds(k * chunk, chunk)
            copy = pltpu.make_async_copy(held.at[j, blocks], ref.at[blocks], sems.at[k, j])
            copy.start()
            leaving.append(copy)
    for copy in leaving:
        copy.wait()


def attend_kernel(clusters, together, table_ref, in_ref, out_ref, own_ref, part_ref):
    scale = 1.0 / math.sqrt(DH)
    factor = scale * math.log2(math.e)

    def attend(cs, own_count, near_count):
        lanes = range(len(cs))
        own_src = [[table_ref[c, 1 + p] for p in range(own_count)] for c in cs]
        near_src = [
            [table_ref[lax.rem(c + 1, clusters), 1 + p] for p in range(near_count)] for c in cs
        ]

        def load(which, sources):
            return jnp.concatenate([in_ref[s, which] for s in sources], axis=0)

        k = [load(0, own_src[i] + near_src[i]) for i in lanes]
        w = [load(1, own_src[i] + near_src[i]) for i in lanes]
        g = [load(2, own_src[i]) for i in lanes]
        width = own_count * BLOCK
        q = [x[:width] for x in k]
        ahead = lax.broadcasted_iota(jnp.int32, (width, width), 1) - lax.broadcasted_iota(
            jnp.int32, (width, width), 0
        )
        scores = [dot(k[i], q[i], NT) for i in lanes]
        dprobs = [dot(w[i], g[i], NT) for i in lanes]
        own_scores = [jnp.where(ahead == 0, -1e30, x[:width]) for x in scores]
        if near_count:
            scores = [jnp.concatenate([own_scores[i], scores[i][width:]], axis=0) for i in lanes]
        else:
            scores = own_scores
        top = [jnp.max(x, axis=0, keepdims=True) for x in scores]
        weights = [jnp.exp2((scores[i] - top[i]) * factor) for i in lanes]
        inverse = [1.0 / jnp.sum(x, axis=0, keepdims=True) for x in weights]
        delta = [
            jnp.sum(weights[i] * dprobs[i], axis=0, keepdims=True) * inverse[i] for i in lanes
        ]
        probs = [weights[i] * inverse[i] for i in lanes]
        dscores = [(probs[i] * (dprobs[i] - delta[i])).astype(jnp.bfloat16) for i in lanes]
        grad_q = [dot(dscores[i], k[i], TN) for i in lanes]
        grad_w = [dot(probs[i].astype(jnp.bfloat16), g[i], NN) for i in lanes]
        grad_k = [dot(dscores[i], q[i], NN) for i in lanes]
        for i in lanes:
            for p in range(own_count):
                rows = slice(p * BLOCK, (p + 1) * BLOCK)
                own_ref[0, own_src[i][p]] = (grad_q[i][rows] + grad_k[i][rows]) * scale
                own_ref[1, own_src[i][p]] = grad_w[i][rows]
            for p in range(near_count):
                rows = slice(width + p * BLOCK, width + (p + 1) * BLOCK)
                part_ref[0, near_src[i][p]] = grad_k[i][rows] * scale
                part_ref[1, near_src[i][p]] = grad_w[i][rows]

    for own_count in (1, 2):
        for near_count in (0, 1, 2):
            shape = 3 * own_count + near_count
            first, end = table_ref[shape, 6], table_ref[shape + 1, 6]
            lanes = together[shape - 3]

            @pl.loop(0, lax.div(end - first + (lanes - 1), lanes))
            def _(turn):
                at = [jnp.minimum(first + turn * lanes + i, end - 1) for i in range(lanes)]
                attend([table_ref[a, 5] for a in at], own_count, near_count)

    @pl.loop(0, clusters, unroll=True)
    def _(c):
        for p in range(2):
            source = table_ref[c, 1 + p]

            @pl.when(table_ref[c, 0] > p)
            def _():
                for j in range(2):
                    part = jnp.where(table_ref[c, 4] > p, part_ref[j, source], 0.0)
                    out_ref[source, j] = (own_ref[j, source] + part).astype(jnp.bfloat16)


def per_device(shared_qk, values, cotangent, cluster_ids, neighbour):
    n_seq = lax.axis_size("seq")
    tokens, lanes = shared_qk.shape
    per_source = tokens // BLOCK
    group_size = neighbour.shape[0] // n_seq
    dtype = shared_qk.dtype
    any_space = pl.BlockSpec(memory_space=pl.ANY)
    smem = pl.BlockSpec(memory_space=pltpu.SMEM)
    vmem = pl.BlockSpec(memory_space=pltpu.VMEM)

    sent, table = pl.pallas_call(
        functools.partial(pack_kernel, PACK, group_size),
        out_shape=(
            jax.ShapeDtypeStruct((n_seq, 3, BLOCK, lanes), dtype),
            jax.ShapeDtypeStruct((group_size, 128), jnp.int32),
        ),
        in_specs=[any_space] * 6,
        out_specs=(any_space, any_space),
        scratch_shapes=[
            pltpu.SMEM(cluster_ids.shape, jnp.int32),
            pltpu.VMEM((1, cluster_ids.shape[0]), jnp.int32),
            pltpu.VMEM((1, neighbour.shape[0]), jnp.int32),
            pltpu.VMEM((group_size, 128), jnp.int32),
            pltpu.VMEM((per_source, 3, BLOCK, lanes), dtype),
            pltpu.SemaphoreType.DMA((4,)),
            pltpu.SemaphoreType.DMA((per_source // PACK, 3)),
            pltpu.SemaphoreType.DMA((per_source,)),
        ],
        name="pack",
    )(
        cluster_ids,
        cluster_ids.reshape(1, -1),
        neighbour.reshape(1, -1),
        *(x.reshape(-1, BLOCK, lanes) for x in (shared_qk, values, cotangent)),
    )
    arrived = lax.all_to_all(sent, "seq", split_axis=0, concat_axis=0, tiled=True)

    returned = pl.pallas_call(
        functools.partial(attend_kernel, group_size, TOGETHER),
        out_shape=jax.ShapeDtypeStruct((n_seq, 2, BLOCK, lanes), dtype),
        in_specs=[smem, vmem],
        out_specs=vmem,
        scratch_shapes=[
            pltpu.VMEM((2, n_seq, BLOCK, lanes), jnp.float32),
            pltpu.VMEM((2, n_seq, BLOCK, lanes), jnp.float32),
        ],
        compiler_params=pltpu.CompilerParams(vmem_limit_bytes=32 * 1024 * 1024),
        name="attend",
    )(table, arrived)
    home = lax.all_to_all(returned, "seq", split_axis=0, concat_axis=0, tiled=True)

    out = jax.ShapeDtypeStruct((per_source, BLOCK, lanes), dtype)
    grads = pl.pallas_call(
        functools.partial(unpack_kernel, UNPACK, group_size),
        out_shape=(out, out),
        in_specs=[smem, vmem],
        out_specs=(any_space, any_space),
        scratch_shapes=[
            pltpu.VMEM((2, per_source, BLOCK, lanes), dtype),
            pltpu.SemaphoreType.DMA((per_source // UNPACK, 2)),
        ],
        compiler_params=pltpu.CompilerParams(vmem_limit_bytes=8 * 1024 * 1024),
        name="unpack",
    )(cluster_ids, home)
    return tuple(x.reshape(tokens, lanes) for x in grads)


def solution(mesh):
    in_specs = (P("seq", "head"), P("seq", "head"), P("seq", "head"), P(), P())
    out_specs = (P("seq", "head"), P("seq", "head"))
    return jax.shard_map(
        per_device, mesh=mesh, in_specs=in_specs, out_specs=out_specs, check_vma=False
    )
```

time: 95.3 us -> 94.2 us (0.988)
  blocking collectives: 33.3 us -> 83.4 us
  waiting for transfers between devices: 36.5 us -> 0 us
  starting transfers between devices: 10.6 us -> 0 us
  other arithmetic: 2.04 us -> 0 us
  Pallas kernels: 11.2 us -> 9.86 us
    all_to_all x0 -> x1, blocking collectives: none -> 50.4 us  [per_device(): lax.all_to_all(sent, 'seq', split_axis=0, concat_axis=0, tiled=True)]
    all_to_all x1 -> x0, waiting for transfers between devices: 36.5 us -> none  [per_device(): lax.all_to_all(sent, 'seq', split_axis=0, concat_axis=0, tiled=True)]
    all_to_all x1 -> x0, starting transfers between devices: 10.6 us -> none  [per_device(): lax.all_to_all(sent, 'seq', split_axis=0, concat_axis=0, tiled=True)]
  transfers between devices with their start and end apart: 1 -> 0, of which waited for: 1 -> 0; matrix products, arithmetic and copies ran while one was open for 3% -> 0% of each run, Pallas kernels for 0% -> 0%
where the time goes in v5:
time: 94.2 us; the launch traced here: 93.9 us
  blocking collectives  83.4 us (89%)
  Pallas kernels  9.86 us (10%)
    all_to_all x1, blocking collectives, per_device(): lax.all_to_all(sent, 'seq', split_axis=0, concat_axis=0, tiled=True)  50.4 us
    all_to_all x1, blocking collectives, per_device(): lax.all_to_all(returned, 'seq', split_axis=0, concat_axis=0, tiled=True)  33 us
    pallas_call x1, Pallas kernels, per_device(): pl.pallas_call(functools.partial(attend_kernel, group_size, TOGETHER), ou...  5.66 us
    pallas_call x1, Pallas kernels, per_device(): pl.pallas_call(functools.partial(pack_kernel, PACK, group_size), out_shap...  2.6 us

profile of v5, /device:TPU:1, one launch (start us, length us, event | category | flops | bytes accessed | tf_op | source)
XLA Modules:
  0.0 93.9 jit_solution(3282256758103091847)
XLA Ops:
  0.6 2.6 %pack.1 = (bf16[32,3,128,128]{3,2,1,0:T(8,128)(2,1)}, s32[16,128]{1,0:T(8,128)}) custom-call(s32[512]{0:T(512)} %ids_ref.3, s32[1,512]{1,0:T(1,128)} %bitcast.7, s32[1,512]{1,0:T(1,128)} %bitcast.11, bf16[16,128,128]{2,1,0:T(8,128)(2,1)} %bitcast.8, bf16[16,128,128]{2,1,0:T(8,128)(2,1)} %bitcast.9, bf16[16,128,128]{2,1,0:T(8,128)(2,1)} %bitcast.10), custom_call_target="tpu_custom_call" | custom-call | tf_op jit(solution)/shard_map/pack/pallas_call | solution.py:215
  3.2 0.0 copy-start.1
  3.3 50.4 %all_to_all.10.in_ref = bf16[32,3,128,128]{3,2,1,0:T(8,128)(2,1)S(1)} all-to-all(bf16[32,3,128,128]{3,2,1,0:T(8,128)(2,1)} %get-tuple-element.7), channel_id=1, replica_groups=mesh['seq'=32,'head'=16] {'seq'}, dimensions={0} | all-to-all | bytes 6291456 | tf_op jit(solution)/shard_map/all_to_all | solution.py:240
  53.6 0.0 copy-done.1
  53.6 5.7 %attend.1 = bf16[32,2,128,128]{3,2,1,0:T(8,128)(2,1)S(1)} custom-call(s32[16,128]{1,0:T(8,128)S(1)} %copy-done.1, bf16[32,3,128,128]{3,2,1,0:T(8,128)(2,1)S(1)} %all_to_all.10.in_ref), custom_call_target="tpu_custom_call" | custom-call | tf_op jit(solution)/shard_map/attend/pallas_call | solution.py:242
  59.3 0.0 copy-start
  59.3 33.0 %all_to_all.11.in_ref = bf16[32,2,128,128]{3,2,1,0:T(8,128)(2,1)S(1)} all-to-all(bf16[32,2,128,128]{3,2,1,0:T(8,128)(2,1)S(1)} %attend.1), channel_id=1, replica_groups=mesh['seq'=32,'head'=16] {'seq'}, dimensions={0} | all-to-all | bytes 4194304 | tf_op jit(solution)/shard_map/all_to_all | solution.py:254
  92.3 0.0 copy-done
  92.3 1.6 %unpack.1 = (bf16[16,128,128]{2,1,0:T(8,128)(2,1)}, bf16[16,128,128]{2,1,0:T(8,128)(2,1)}) custom-call(s32[512]{0:T(512)S(1)} %copy-done, bf16[32,2,128,128]{3,2,1,0:T(8,128)(2,1)S(1)} %all_to_all.11.in_ref), custom_call_target="tpu_custom_call" | custom-call | tf_op jit(solution)/shard_map/unpack/pallas_call | solution.py:257
Async XLA Ops:
  3.2 50.4 %copy-start.1 = (s32[16,128]{1,0:T(8,128)S(1)}, s32[16,128]{1,0:T(8,128)}, u32[]{:S(2)}) copy-start(s32[16,128]{1,0:T(8,128)} %get-tuple-element.6.table_ref) | copy-start | bytes 24580
  59.3 33.0 %copy-start = (s32[512]{0:T(512)S(1)}, s32[512]{0:T(512)}, u32[]{:S(2)}) copy-start(s32[512]{0:T(512)} %ids_ref.3) | copy-start | bytes 6148

commit v6 on v5

--- a/solution.py
+++ b/solution.py
@@ -166,9 +166,9 @@
         ]
         probs = [weights[i] * inverse[i] for i in lanes]
         dscores = [(probs[i] * (dprobs[i] - delta[i])).astype(jnp.bfloat16) for i in lanes]
-        grad_q = [dot(dscores[i], k[i], TN) for i in lanes]
         grad_w = [dot(probs[i].astype(jnp.bfloat16), g[i], NN) for i in lanes]
         grad_k = [dot(dscores[i], q[i], NN) for i in lanes]
+        grad_q = [dot(dscores[i], k[i], TN) for i in lanes]
         for i in lanes:
             for p in range(own_count):
                 rows = slice(p * BLOCK, (p + 1) * BLOCK)
@@ -185,10 +185,17 @@
             first, end = table_ref[shape, 6], table_ref[shape + 1, 6]
             lanes = together[shape - 3]
 
-            @pl.loop(0, lax.div(end - first + (lanes - 1), lanes))
+            whole = lax.div(end - first, lanes)
+            rest = end - first - whole * lanes
+
+            @pl.loop(0, whole + (rest > 1).astype(jnp.int32))
             def _(turn):
                 at = [jnp.minimum(first + turn * lanes + i, end - 1) for i in range(lanes)]
                 attend([table_ref[a, 5] for a in at], own_count, near_count)
+
+            @pl.when(rest == 1)
+            def _():
+                attend([table_ref[end - 1, 5]], own_count, near_count)
 
     @pl.loop(0, clusters, unroll=True)
     def _(c):

time: 94.2 us -> 92.9 us (0.986)
  no operation moved by 1% of the time
where the time goes in v6:
time: 92.9 us; the launch traced here: 92.7 us
  blocking collectives  82.7 us (89%)
  Pallas kernels  9.24 us (10%)
    all_to_all x1, blocking collectives, per_device(): lax.all_to_all(sent, 'seq', split_axis=0, concat_axis=0, tiled=True)  50.4 us
    all_to_all x1, blocking collectives, per_device(): lax.all_to_all(returned, 'seq', split_axis=0, concat_axis=0, tiled=True)  32.4 us
    pallas_call x1, Pallas kernels, per_device(): pl.pallas_call(functools.partial(attend_kernel, group_size, TOGETHER), ou...  5.04 us
    pallas_call x1, Pallas kernels, per_device(): pl.pallas_call(functools.partial(pack_kernel, PACK, group_size), out_shap...  2.6 us

profile of v6, /device:TPU:1, one launch (start us, length us, event | category | flops | bytes accessed | tf_op | source)
XLA Modules:
  0.0 92.7 jit_solution(16099486736518199524)
XLA Ops:
  0.6 2.6 %pack.1 = (bf16[32,3,128,128]{3,2,1,0:T(8,128)(2,1)}, s32[16,128]{1,0:T(8,128)}) custom-call(s32[512]{0:T(512)} %ids_ref.3, s32[1,512]{1,0:T(1,128)} %bitcast.7, s32[1,512]{1,0:T(1,128)} %bitcast.11, bf16[16,128,128]{2,1,0:T(8,128)(2,1)} %bitcast.8, bf16[16,128,128]{2,1,0:T(8,128)(2,1)} %bitcast.9, bf16[16,128,128]{2,1,0:T(8,128)(2,1)} %bitcast.10), custom_call_target="tpu_custom_call" | custom-call | tf_op jit(solution)/shard_map/pack/pallas_call | solution.py:222
  3.2 0.0 copy-start.1
  3.3 50.4 %all_to_all.10.in_ref = bf16[32,3,128,128]{3,2,1,0:T(8,128)(2,1)S(1)} all-to-all(bf16[32,3,128,128]{3,2,1,0:T(8,128)(2,1)} %get-tuple-element.7), channel_id=1, replica_groups=mesh['seq'=32,'head'=16] {'seq'}, dimensions={0} | all-to-all | bytes 6291456 | tf_op jit(solution)/shard_map/all_to_all | solution.py:247
  53.6 0.0 copy-done.1
  53.6 5.0 %attend.1 = bf16[32,2,128,128]{3,2,1,0:T(8,128)(2,1)S(1)} custom-call(s32[16,128]{1,0:T(8,128)S(1)} %copy-done.1, bf16[32,3,128,128]{3,2,1,0:T(8,128)(2,1)S(1)} %all_to_all.10.in_ref), custom_call_target="tpu_custom_call" | custom-call | tf_op jit(solution)/shard_map/attend/pallas_call | solution.py:249
  58.7 0.0 copy-start
  58.7 32.4 %all_to_all.11.in_ref = bf16[32,2,128,128]{3,2,1,0:T(8,128)(2,1)S(1)} all-to-all(bf16[32,2,128,128]{3,2,1,0:T(8,128)(2,1)S(1)} %attend.1), channel_id=1, replica_groups=mesh['seq'=32,'head'=16] {'seq'}, dimensions={0} | all-to-all | bytes 4194304 | tf_op jit(solution)/shard_map/all_to_all | solution.py:261
  91.1 0.0 copy-done
  91.1 1.6 %unpack.1 = (bf16[16,128,128]{2,1,0:T(8,128)(2,1)}, bf16[16,128,128]{2,1,0:T(8,128)(2,1)}) custom-call(s32[512]{0:T(512)S(1)} %copy-done, bf16[32,2,128,128]{3,2,1,0:T(8,128)(2,1)S(1)} %all_to_all.11.in_ref), custom_call_target="tpu_custom_call" | custom-call | tf_op jit(solution)/shard_map/unpack/pallas_call | solution.py:264
Async XLA Ops:
  3.2 50.4 %copy-start.1 = (s32[16,128]{1,0:T(8,128)S(1)}, s32[16,128]{1,0:T(8,128)}, u32[]{:S(2)}) copy-start(s32[16,128]{1,0:T(8,128)} %get-tuple-element.6.table_ref) | copy-start | bytes 24580
  58.7 32.4 %copy-start = (s32[512]{0:T(512)S(1)}, s32[512]{0:T(512)}, u32[]{:S(2)}) copy-start(s32[512]{0:T(512)} %ids_ref.3) | copy-start | bytes 6148

commit v7 on v6

--- a/solution.py
+++ b/solution.py
@@ -53,9 +53,15 @@
     rank = count((shape_row < shape) | ((shape_row == shape) & (j < i)))
     order = picked(j, as_row(rank) == i)
     starts = count(shape_row < i)
+    held_row = as_row(held)
+    start_row = as_row(picked(held_row, j < i))
+    nth = i - start_row
+    mine = (nth >= 0) & (nth < held_row)
+    block_source = picked(jnp.where(nth == 0, as_row(low), as_row(high)), mine)
+    block_part = count(mine & (as_row(part) > nth))
     place = lax.broadcasted_iota(jnp.int32, table_ref.shape, 1)
     table = jnp.zeros(table_ref.shape, jnp.int32)
-    for k, column in enumerate((held, low, high, near, part, order, starts)):
+    for k, column in enumerate((held, low, high, near, block_part, order, starts, block_source)):
         table = jnp.where(place == k, column, table)
     table_ref[...] = table
 
@@ -198,15 +204,11 @@
                 attend([table_ref[end - 1, 5]], own_count, near_count)
 
     @pl.loop(0, clusters, unroll=True)
-    def _(c):
-        for p in range(2):
-            source = table_ref[c, 1 + p]
-
-            @pl.when(table_ref[c, 0] > p)
-            def _():
-                for j in range(2):
-                    part = jnp.where(table_ref[c, 4] > p, part_ref[j, source], 0.0)
-                    out_ref[source, j] = (own_ref[j, source] + part).astype(jnp.bfloat16)
+    def _(r):
+        source = table_ref[r, 7]
+        for j in range(2):
+            part = jnp.where(table_ref[r, 4] > 0, part_ref[j, source], 0.0)
+            out_ref[source, j] = (own_ref[j, source] + part).astype(jnp.bfloat16)
 
 
 def per_device(shared_qk, values, cotangent, cluster_ids, neighbour):

time: 92.9 us -> 92.8 us (level)
  no operation moved by 1% of the time
where the time goes in v7:
time: 92.8 us; the launch traced here: 92.7 us
  blocking collectives  82.4 us (89%)
  Pallas kernels  9.66 us (10%)
    all_to_all x1, blocking collectives, per_device(): lax.all_to_all(sent, 'seq', split_axis=0, concat_axis=0, tiled=True)  50.4 us
    all_to_all x1, blocking collectives, per_device(): lax.all_to_all(returned, 'seq', split_axis=0, concat_axis=0, tiled=True)  32 us
    pallas_call x1, Pallas kernels, per_device(): pl.pallas_call(functools.partial(attend_kernel, group_size, TOGETHER), ou...  5.45 us
    pallas_call x1, Pallas kernels, per_device(): pl.pallas_call(functools.partial(pack_kernel, PACK, group_size), out_shap...  2.62 us

profile of v7, /device:TPU:1, one launch (start us, length us, event | category | flops | bytes accessed | tf_op | source)
XLA Modules:
  0.0 92.7 jit_solution(1986726880889562074)
XLA Ops:
  0.6 2.6 %pack.1 = (bf16[32,3,128,128]{3,2,1,0:T(8,128)(2,1)}, s32[16,128]{1,0:T(8,128)}) custom-call(s32[512]{0:T(512)} %ids_ref.3, s32[1,512]{1,0:T(1,128)} %bitcast.7, s32[1,512]{1,0:T(1,128)} %bitcast.11, bf16[16,128,128]{2,1,0:T(8,128)(2,1)} %bitcast.8, bf16[16,128,128]{2,1,0:T(8,128)(2,1)} %bitcast.9, bf16[16,128,128]{2,1,0:T(8,128)(2,1)} %bitcast.10), custom_call_target="tpu_custom_call" | custom-call | tf_op jit(solution)/shard_map/pack/pallas_call | solution.py:224
  3.3 0.0 copy-start.1
  3.3 50.4 %all_to_all.10.in_ref = bf16[32,3,128,128]{3,2,1,0:T(8,128)(2,1)S(1)} all-to-all(bf16[32,3,128,128]{3,2,1,0:T(8,128)(2,1)} %get-tuple-element.7), channel_id=1, replica_groups=mesh['seq'=32,'head'=16] {'seq'}, dimensions={0} | all-to-all | bytes 6291456 | tf_op jit(solution)/shard_map/all_to_all | solution.py:249
  53.6 0.0 copy-done.1
  53.6 5.5 %attend.1 = bf16[32,2,128,128]{3,2,1,0:T(8,128)(2,1)S(1)} custom-call(s32[16,128]{1,0:T(8,128)S(1)} %copy-done.1, bf16[32,3,128,128]{3,2,1,0:T(8,128)(2,1)S(1)} %all_to_all.10.in_ref), custom_call_target="tpu_custom_call" | custom-call | tf_op jit(solution)/shard_map/attend/pallas_call | solution.py:251
  59.1 0.0 copy-start
  59.1 32.0 %all_to_all.11.in_ref = bf16[32,2,128,128]{3,2,1,0:T(8,128)(2,1)S(1)} all-to-all(bf16[32,2,128,128]{3,2,1,0:T(8,128)(2,1)S(1)} %attend.1), channel_id=1, replica_groups=mesh['seq'=32,'head'=16] {'seq'}, dimensions={0} | all-to-all | bytes 4194304 | tf_op jit(solution)/shard_map/all_to_all | solution.py:263
  91.1 0.0 copy-done
  91.1 1.6 %unpack.1 = (bf16[16,128,128]{2,1,0:T(8,128)(2,1)}, bf16[16,128,128]{2,1,0:T(8,128)(2,1)}) custom-call(s32[512]{0:T(512)S(1)} %copy-done, bf16[32,2,128,128]{3,2,1,0:T(8,128)(2,1)S(1)} %all_to_all.11.in_ref), custom_call_target="tpu_custom_call" | custom-call | tf_op jit(solution)/shard_map/unpack/pallas_call | solution.py:266
Async XLA Ops:
  3.3 50.4 %copy-start.1 = (s32[16,128]{1,0:T(8,128)S(1)}, s32[16,128]{1,0:T(8,128)}, u32[]{:S(2)}) copy-start(s32[16,128]{1,0:T(8,128)} %get-tuple-element.6.table_ref) | copy-start | bytes 24580
  59.1 32.1 %copy-start = (s32[512]{0:T(512)S(1)}, s32[512]{0:T(512)}, u32[]{:S(2)}) copy-start(s32[512]{0:T(512)} %ids_ref.3) | copy-start | bytes 6148
